TPU v7x, 32 devices: a whole 2x2x4 slice. The times are simulated.
32 devices in a mesh: head: 4 (over y, x), ctx: 8 (over z, core).
Axes of the slice: x: 2, y: 2, z: 4, core: 2. Of those that a mesh axis runs over, the one named last changes fastest.
Arguments:
- queries: bfloat16 [8, 512, 8192], P('ctx', 'head'), may hold values from -6 to 6
- keys: bfloat16 [8, 512, 8192], P('ctx', 'head'), may hold values from -6 to 6
- values: bfloat16 [8, 512, 8192], P('ctx', 'head'), may hold values from -6 to 6
- gate: bfloat16 [8, 512, 8192], P('ctx', 'head'), may hold values from -6 to 6
- log_decay: float32 [8, 64, 512], P('ctx', 'head'), may hold values from -1 to 0, as said below
- norm_gain: bfloat16 [8192], P('head'), may hold values from 0.099609375 to 1.8984375
Outputs:
- attended: bfloat16 [8, 512, 8192], P('ctx', 'head')
Inputs may be any that keep to these rules, and one draw needn't show every extreme that they name: `log_decay`: every entry is negative.
All inputs are finite; a program needn't handle non-finite values.
Results may differ from a plain program's by a relative error of at most 0.0048.
Values may be sent and summed in bfloat16 or wider, within the bound.
No kernel may reach another device: no remote copies, remote signals or barrier semaphores. Data moves between devices by JAX's collectives and lax.ppermute only.
A program may use at most 192 MiB of HBM per device.

v0:
```python
import functools

import jax
import jax.numpy as jnp
from jax import lax
from jax.experimental import pallas as pl
from jax.experimental.pallas import tpu as pltpu
from jax.sharding import Mesh
from jax.sharding import PartitionSpec as P

GROUPS = 2
STEP = 8
EXTRA = 16
VMEM_LIMIT = 8 * 1024 * 1024
NN = (((1,), (0,)), ((), ()))
NT = (((1,), (1,)), ((), ()))
TN = (((0,), (0,)), ((), ()))


def dot(a, b, dims, precision=None):
    return lax.dot_general(a, b, dims, precision=precision, preferred_element_type=jnp.float32)


def split(value):
    first = value.astype(jnp.bfloat16)
    left = value - first.astype(jnp.float32)
    second = left.astype(jnp.bfloat16)
    return first, second, (left - second.astype(jnp.float32)).astype(jnp.bfloat16)


def sums_over(decay, keep):
    heads, length = decay.shape
    rows = lax.broadcasted_iota(jnp.int32, (length, length), 0)
    columns = lax.broadcasted_iota(jnp.int32, (length, length), 1)
    chosen = jnp.where(keep(rows, columns), 1.0, 0.0).astype(jnp.bfloat16)
    parts = [part.astype(jnp.float32) for part in split(decay)]
    both = dot(jnp.concatenate(parts, axis=0).astype(jnp.bfloat16), chosen, NN)
    return both[:heads] + (both[heads : 2 * heads] + both[2 * heads :])


def join(rows, head):
    wide = rows.astype(jnp.float32)
    return wide[3 * head : 3 * head + 1] + (
        wide[3 * head + 1 : 3 * head + 2] + wide[3 * head + 2 : 3 * head + 3]
    )


def decay_rows(totals):
    parts = [part for total in totals for part in split(total)]
    blank = jnp.zeros((EXTRA - len(parts), totals[0].shape[1]), jnp.bfloat16)
    return jnp.concatenate(parts + [blank], axis=0)


def pack_kernel(parts, decay_ref, packed_ref):
    length = packed_ref.shape[2]
    for place in range(packed_ref.shape[0]):
        start = place % parts * length
        packed_ref[place] = decay_ref[0, :, start : start + length]


def gate_kernel(half, begin, share, dim, me_ref, gate_ref, *refs):
    *results, done_ref, copy_ref, result_ref, done = refs[-6:]
    width = share * dim
    loads, stores = [], []
    for at, out_ref in enumerate(results):
        first = (me_ref[1] if at == 0 else 1 - me_ref[1]) * half + begin
        columns = pl.ds(pl.multiple_of(first * dim, width), width)
        loads.append(pltpu.make_async_copy(gate_ref.at[0, :, columns], copy_ref.at[at], done.at[at]))
        stores.append(pltpu.make_async_copy(result_ref.at[at], out_ref, done.at[2 + at]))
        loads[-1].start()
    for at in range(len(results)):
        loads[at].wait()
        for head in range(share):
            c = slice(head * dim, (head + 1) * dim)
            turned = jnp.tanh(0.5 * copy_ref[at, :, c].astype(jnp.float32))
            result_ref[at, :, c] = 0.5 + 0.5 * turned
        stores[at].start()
    done_ref[...] = jnp.zeros_like(done_ref)
    for store in stores:
        store.wait()


def heads_at(first, head, dim):
    return pl.ds(pl.multiple_of((first + head) * dim, dim), dim)


def decays_at(decay_ref, block, first):
    local = decay_ref.shape[1]
    parts = decay_ref.shape[0] // 2
    rows = pl.ds(pl.multiple_of(first % local, STEP), STEP)
    return decay_ref[block * parts + first // local, rows, :]


def load_kernel(half, begin, count, dim, me_ref, *refs):
    sources, copies, done = refs[:2], refs[-3:-1], refs[-1]
    width = count * dim
    columns = pl.ds(pl.multiple_of((me_ref[1] * half + begin) * dim, width), width)
    moves = [
        pltpu.make_async_copy(source.at[0, :, columns], copy, done.at[at])
        for at, (source, copy) in enumerate(zip(sources, copies))
    ]
    for move in moves:
        move.start()
    for move in moves:
        move.wait()


def state_kernel(dim, owned, half, begin, masks, loaded, me_ref, decay_ref, *refs):
    arrays = refs[:4]
    stacked_ref, copy_ref, done = refs[-3:]
    slots = refs[-3 - 2 * len(masks) : -3]
    part, core = me_ref[0], me_ref[1]
    turns = [(part >> 1) ^ mask for mask in masks]
    firsts = [core * half + begin + turn * STEP for turn in turns]
    width = STEP * dim
    moves = {}
    for at in range(2 if loaded else 0, 4):
        for turn, first in enumerate(firsts):
            columns = pl.ds(pl.multiple_of(first * dim, width), width)
            moves[at, turn] = pltpu.make_async_copy(
                arrays[at].at[0, :, columns], copy_ref.at[turn, at], done.at[turn, at]
            )
            moves[at, turn].start()

    def piece(turn, at, head):
        if loaded and at < 2:
            return arrays[at][:, heads_at(turns[turn] * STEP, head, dim)]
        return copy_ref[turn, at, :, head * dim : (head + 1) * dim]

    for source in range(2):
        block = core if source == 0 else 1 - core
        for turn, first in enumerate(firsts):
            decay = decays_at(decay_ref, block, first)
            weight = jnp.exp(sums_over(decay, lambda u, s: u > s))
            whole = jnp.broadcast_to(jnp.sum(decay, axis=1, keepdims=True), (STEP, dim))
            for at in (2 * source, 2 * source + 1):
                if (at, turn) in moves:
                    moves[at, turn].wait()
            states = []
            for head in range(STEP):
                decayed = piece(turn, 2 * source, head).T.astype(jnp.float32)
                decayed = (decayed * weight[head : head + 1, :]).astype(jnp.bfloat16)
                states.append(dot(decayed, piece(turn, 2 * source + 1, head), NN))
            for head in range(STEP):
                owner, spot = divmod(head, owned)
                span = slice(spot * dim, (spot + 1) * dim)
                stacked_ref[turn, owner, block, span, :] = states[head].astype(jnp.bfloat16)
            for at in range(2):
                stacked_ref[turn, at, block, owned * dim :, :] = decay_rows(
                    [whole[head : head + 1] for head in range(at * owned, (at + 1) * owned)]
                )
    for turn in range(len(masks)):
        for at in range(2):
            slots[2 * turn + at][...] = stacked_ref[turn, (part & 1) ^ at]


def inside_kernel(
    dim, half, begin, count, other, me_ref, queries_ref, keys_ref, values_ref, decay_ref, *rest
):
    inside_ref, down_ref, done_ref = rest[-3:]
    core = me_ref[1]
    length = decay_ref.shape[2]
    rows = lax.broadcasted_iota(jnp.int32, (length, length), 0)
    causal = rows >= lax.broadcasted_iota(jnp.int32, (length, length), 1)
    for turn in range(count // STEP):
        first = (1 - core if other else core) * half + begin + turn * STEP
        decay = decays_at(decay_ref, core, first)
        across = sums_over(decay, lambda u, s: u <= s)
        down = across.T
        down_ref[turn] = jnp.exp(down)
        columns = [heads_at(first, head, dim) for head in range(STEP)]
        scores = [dot(queries_ref[0, :, c], keys_ref[0, :, c], NT) for c in columns]
        weights = []
        for head in range(STEP):
            gap = down[:, head : head + 1] - across[head : head + 1, :]
            weight = scores[head] * jnp.exp(jnp.where(causal, gap, -jnp.inf))
            weights.append(weight.astype(jnp.bfloat16))
        for head, c in enumerate(columns):
            at = (turn * STEP + head) * dim
            inside_ref[:, at : at + dim] = dot(weights[head], values_ref[0, :, c], NN)
    done_ref[...] = jnp.zeros_like(done_ref)


def gather_states(part, slots, stacked_ref):
    parts = len(slots)
    for slot, slot_ref in enumerate(slots):
        for block in range(2):
            stacked_ref[block * parts + (part ^ slot)] = slot_ref[block]


def total_kernel(dim, owned, parts, me_ref, *refs):
    total_ref, stacked_ref = refs[-2:]
    gather_states(me_ref[0], refs[:parts], stacked_ref)
    count = 2 * parts
    extra = [stacked_ref[at, owned * dim :, :] for at in range(count)]
    sums = []
    for head in range(owned):
        span = slice(head * dim, (head + 1) * dim)
        after = jnp.zeros((1, dim), jnp.float32)
        total = stacked_ref[count - 1, span, :].astype(jnp.float32)
        for at in range(count - 2, -1, -1):
            after += join(extra[at + 1], head)
            total += jnp.exp(after) * stacked_ref[at, span, :].astype(jnp.float32)
        total_ref[span, :] = total.astype(jnp.bfloat16)
        sums.append(after + join(extra[0], head))
    total_ref[owned * dim :, :] = decay_rows(sums)


def widen_kernel(dim, owned, step, me_ref, mine_ref, other_ref, *refs):
    out_ref = refs[-1]
    later = (me_ref[2] >> step) % 2 == 1
    extra = mine_ref[owned * dim :, :], other_ref[owned * dim :, :]
    sums = []
    for head in range(owned):
        span = slice(head * dim, (head + 1) * dim)
        mine, other = join(extra[0], head), join(extra[1], head)
        total = jnp.where(later, 1.0, jnp.exp(other)) * mine_ref[span, :].astype(jnp.float32)
        total += jnp.where(later, jnp.exp(mine), 1.0) * other_ref[span, :].astype(jnp.float32)
        out_ref[span, :] = total.astype(jnp.bfloat16)
        sums.append(mine + other)
    out_ref[owned * dim :, :] = decay_rows(sums)


def prefix_kernel(dim, owned, parts, stretches, me_ref, gain_ref, *refs):
    stacked_ref, prefix_ref = refs[-2:]
    slots, totals = refs[:parts], refs[parts : parts + stretches]
    count = 2 * parts
    results = refs[-2 - parts : -2]
    gather_states(me_ref[0], slots, stacked_ref)
    extra = [stacked_ref[at, owned * dim :, :] for at in range(count)]
    more = [total_ref[owned * dim :, :] for total_ref in totals]
    earlier = [
        ((me_ref[2] >> step) % 2).astype(jnp.float32) for step in range(len(totals))
    ]
    for head in range(owned):
        span = slice(head * dim, (head + 1) * dim)
        prefix = jnp.zeros((dim, dim), jnp.float32)
        after = jnp.zeros((1, dim), jnp.float32)
        for turn, total_ref in enumerate(totals):
            factor = earlier[turn] * jnp.exp(after)
            prefix += factor * total_ref[span, :].astype(jnp.float32)
            after += earlier[turn] * join(more[turn], head)
        for at in range(count):
            prefix_ref[at, span, :] = prefix.astype(jnp.bfloat16)
            if at < count - 1:
                prefix = jnp.exp(join(extra[at], head)) * prefix
                prefix += stacked_ref[at, span, :].astype(jnp.float32)
    size = owned * dim
    for slot, result_ref in enumerate(results):
        for block in range(2):
            result_ref[block * size : (block + 1) * size, :] = prefix_ref[
                block * parts + (me_ref[0] ^ slot)
            ]
        if result_ref.shape[0] > 2 * size:
            result_ref[2 * size :, :] = gain_ref[...]


def merge_kernel(parts, me_ref, *refs):
    slots, gain_ref, prefix_ref = refs[:parts], refs[-2], refs[-1]
    others = refs[-4:-2]
    size = prefix_ref.shape[1]
    local = gain_ref.shape[0] // parts
    block = 1 - me_ref[1]
    for slot, slot_ref in enumerate(slots):
        owner = me_ref[0] ^ slot
        prefix_ref[owner] = slot_ref[pl.ds(pl.multiple_of(block * size, size), size), :]
        if slot_ref.shape[0] > 2 * size:
            rows = pl.ds(pl.multiple_of(owner * local, local), local)
            gain_ref[rows, :] = slot_ref[2 * size :, :].astype(jnp.float32)
    if slots[0].shape[0] == 2 * size:
        gain_ref[...] = jnp.zeros_like(gain_ref)
    each = parts // len(others)
    for turn, other_ref in enumerate(others):
        other_ref[...] = prefix_ref[turn * each : (turn + 1) * each]


def output_kernel(
    dim, owned, half, begin, masks, other, me_ref,
    queries_ref, inside_ref, down_ref, gate_ref, gains, *refs,
):
    out_ref, done_ref, prefix_ref, result_ref, sent = refs[-5:]
    part, core = me_ref[0], me_ref[1]
    size = owned * dim
    if other:
        turns, prefixes = [0, 1], [refs[0], refs[1]]
    else:
        turns = [(part >> 1) ^ mask for mask in masks]
        prefixes = [prefix_ref.at[turn] for turn in range(len(masks))]
        rows = pl.ds(pl.multiple_of(core * size, size), size)
        for turn in range(len(masks)):
            for at in range(2):
                prefix_ref[turn, (part & 1) ^ at] = refs[2 * turn + at][rows, :]
    blocks = [lax.broadcasted_iota(jnp.int32, (2 * dim, 2 * dim), axis) // dim for axis in (0, 1)]
    average = jnp.where(blocks[0] == blocks[1], 1.0 / dim, 0.0).astype(jnp.bfloat16)
    moves = []
    for at, turn in enumerate(turns):
        first = (1 - core if other else core) * half + begin + turn * STEP
        gain = gains[pl.ds(pl.multiple_of(first, STEP), STEP), :]
        down = down_ref[turn]
        columns = [heads_at(first, head, dim) for head in range(STEP)]
        here = [heads_at(turn * STEP, head, dim) for head in range(STEP)]
        carried = []
        for head, c in enumerate(columns):
            owner, spot = divmod(head, owned)
            prefix = prefixes[at][owner, spot * dim : (spot + 1) * dim, :]
            carried.append(dot(queries_ref[0, :, c], prefix, NN))
        mixed, means = [], []
        for head in range(STEP):
            mixed.append(inside_ref[:, here[head]] + carried[head] * down[:, head : head + 1])
        for head in range(0, STEP, 2):
            squares = [(value * value).astype(jnp.bfloat16) for value in mixed[head : head + 2]]
            both = dot(jnp.concatenate(squares, axis=1), average, NN)
            means += [both[:, :dim], both[:, dim:]]
        for head in range(STEP):
            factor = gain[head : head + 1, :] * gate_ref[:, here[head]]
            normed = mixed[head] * lax.rsqrt(means[head] + 1e-06) * factor
            result_ref[at, :, head * dim : (head + 1) * dim] = normed.astype(jnp.bfloat16)
            if head % 2 == 1:
                start = pl.multiple_of((first + head - 1) * dim, 2 * dim)
                moves.append(
                    pltpu.make_async_copy(
                        result_ref.at[at, :, (head - 1) * dim : (head + 1) * dim],
                        out_ref.at[0, :, pl.ds(start, 2 * dim)],
                        sent.at[at, head // 2],
                    )
                )
                moves[-1].start()
    done_ref[...] = jnp.zeros_like(done_ref)
    for move in moves:
        move.wait()


def kernel_call(body, name, in_specs, out_specs, out_shape, scratch=(), aliases={}, cost=0):
    return pl.pallas_call(
        body,
        grid_spec=pltpu.PrefetchScalarGridSpec(
            num_scalar_prefetch=1,
            grid=(),
            in_specs=in_specs,
            out_specs=out_specs,
            scratch_shapes=scratch,
        ),
        out_shape=out_shape,
        input_output_aliases=aliases,
        compiler_params=pltpu.CompilerParams(vmem_limit_bytes=VMEM_LIMIT),
        cost_estimate=pl.CostEstimate(
            flops=int(1e9 * cost) + 1, transcendentals=0, bytes_accessed=1
        ),
        name=name,
    )


def on_device(parts, planes, queries, keys, values, gate, log_decay, norm_gain):
    _, length, width = queries.shape
    local = log_decay.shape[1]
    dim = width // (local * parts)
    count = 2 * parts
    half = local * parts // 2
    owned = half // (GROUPS * parts)
    rows = owned * dim + EXTRA
    me = jnp.stack([lax.axis_index(axis) for axis in ("head", "core", "z")]).astype(jnp.int32)
    swap = [(0, 1), (1, 0)]

    values_other = lax.ppermute(values, "core", swap)
    keys_other = lax.ppermute(keys, "core", swap)
    packed = pl.pallas_call(
        functools.partial(pack_kernel, parts),
        out_shape=jax.ShapeDtypeStruct((count, local, length), jnp.float32),
        name="pack",
    )(log_decay)
    decay = lax.all_to_all(packed, ("core", "head"), 0, 0, tiled=True)
    gain = norm_gain.reshape(local, dim)

    vmem = pl.BlockSpec(memory_space=pltpu.VMEM)
    hbm = pl.BlockSpec(memory_space=pl.ANY)

    def in_vmem(array):
        return pltpu.with_memory_space_constraint(array, pltpu.VMEM)

    def in_hbm(array):
        return pltpu.with_memory_space_constraint(array, pltpu.HBM)

    own = in_hbm(keys), in_hbm(values)
    share = half // GROUPS
    keys, values, queries = (in_vmem(array) for array in (keys, values, queries))

    def exchange(slots):
        arrived = list(slots)
        for slot in sorted(range(1, parts), key=lambda s: -bin(s).count("1")):
            pairs = [(at, at ^ slot) for at in range(parts)]
            arrived[slot] = lax.ppermute(slots[slot], "head", pairs)
        return arrived

    before = ()
    held = []
    state_type = jax.ShapeDtypeStruct((2, rows, dim), jnp.bfloat16)
    token = jax.ShapeDtypeStruct((8, 128), jnp.float32)
    inside = {}

    def inside_part(before, cost=0):
        group, other = divmod(len(inside), 2)
        *inside[group, other], made = kernel_call(
            functools.partial(inside_kernel, dim, half, group * share, share, other),
            f"inside{group}_{other}",
            [vmem] * 4 + [hbm] * len(before),
            [vmem] * 3,
            [
                pltpu.VMEM((length, share * dim), jnp.float32),
                jax.ShapeDtypeStruct((share // STEP, length, STEP), jnp.float32),
                token,
            ],
            cost=cost,
        )(me, queries, keys, values, decay, *before)
        return (made,)

    gate_type = jax.ShapeDtypeStruct((length, share * dim), jnp.float32)
    gates = {}

    def gates_of(group, before):
        gates[group, 0], gates[group, 1], made = kernel_call(
            functools.partial(gate_kernel, half, group * share, share, dim),
            f"gates{group}",
            [hbm] * (1 + len(before)),
            [hbm, hbm, vmem],
            [pltpu.HBM(gate_type.shape, gate_type.dtype)] * 2 + [token],
            [
                pltpu.VMEM((2, length, share * dim), jnp.bfloat16),
                pltpu.VMEM((2,) + gate_type.shape, jnp.float32),
                pltpu.SemaphoreType.DMA((4,)),
            ],
        )(me, in_hbm(gate), *before)
        return (made,)

    first_slices = kernel_call(
        functools.partial(load_kernel, half, 0, share, dim),
        "load",
        [hbm] * 3,
        [vmem] * 2,
        [jax.ShapeDtypeStruct((length, share * dim), jnp.bfloat16)] * 2,
        [pltpu.SemaphoreType.DMA((2,))],
    )(me, *own, packed)
    for group in range(GROUPS):
        slots = {}
        for masks in ((1, 0),):
            loaded = group == 0
            state = kernel_call(
                functools.partial(state_kernel, dim, owned, half, group * share, masks, loaded),
                f"state{group}",
                [vmem] + [vmem if loaded else hbm] * 2 + [hbm] * (2 + len(before)),
                [vmem] * (2 * len(masks)),
                [state_type] * (2 * len(masks)),
                [
                    pltpu.VMEM((len(masks), 2) + state_type.shape, jnp.bfloat16),
                    pltpu.VMEM((len(masks), 4, length, STEP * dim), jnp.bfloat16),
                    pltpu.SemaphoreType.DMA((len(masks), 4)),
                ],
            )(me, decay, *(first_slices if loaded else own), keys_other, values_other, *before)
            before = tuple(state[:1])
            for at, array in enumerate(state):
                slots[2 * masks[at // 2] + at % 2] = array
        held.append(exchange([slots[slot] for slot in range(parts)]))
    before = inside_part(inside_part(before))

    arrived = []
    stacked = pltpu.VMEM((count, rows, dim), jnp.bfloat16)
    total_type = jax.ShapeDtypeStruct((rows, dim), jnp.bfloat16)

    def with_plane(total, step):
        pairs = [(at, at ^ (1 << step)) for at in range(planes)]
        return lax.ppermute(total, "z", pairs)

    def widen(group, step, total, other, before):
        return kernel_call(
            functools.partial(widen_kernel, dim, owned, step),
            f"widen{group}_{step}",
            [vmem] * 2 + [hbm] * len(before),
            vmem,
            total_type,
        )(me, total, other, *before)

    def prefix_of(group, before):
        stretches = arrived[group]
        return kernel_call(
            functools.partial(prefix_kernel, dim, owned, parts, len(stretches)),
            f"prefix{group}",
            [vmem] * (1 + parts + len(stretches)) + [hbm] * len(before),
            [vmem] * parts,
            [prefix_type] * parts,
            [stacked, pltpu.VMEM((count, size, dim), jnp.bfloat16)],
        )(me, gain, *held[group], *stretches, *before)

    size = owned * dim
    prefix_type = jax.ShapeDtypeStruct((2 * size + local, dim), jnp.bfloat16)
    prefixes = []
    for group in range(GROUPS):
        total = kernel_call(
            functools.partial(total_kernel, dim, owned, parts),
            f"total{group}",
            [vmem] * parts + [hbm],
            vmem,
            total_type,
            [stacked],
        )(me, *held[group], *before)
        before = (total,)
        stretches = [with_plane(total, 0)]
        arrived.append(stretches)
        if group > 0:
            prefix = prefix_of(group - 1, before)
            before = tuple(prefix[:1])
            prefixes.append(exchange(prefix))
        if group < GROUPS - 1:
            before = inside_part(before)
        for step in range(1, planes.bit_length() - 1):
            total = widen(group, step - 1, total, stretches[-1], before)
            before = (total,)
            stretches.append(with_plane(total, step))
        while group == GROUPS - 1 and len(inside) < 2 * GROUPS:
            before = inside_part(before, 2)
        before = gates_of(group, before)
    prefix = prefix_of(GROUPS - 1, before)
    before = tuple(prefix[:1])
    prefixes.append(exchange(prefix))

    part_type = jax.ShapeDtypeStruct((parts, size, dim), jnp.bfloat16)
    half_type = jax.ShapeDtypeStruct((parts // 2, size, dim), jnp.bfloat16)
    gain_type = jax.ShapeDtypeStruct((parts * local, dim), jnp.float32)

    def merge(group, before, cost):
        return kernel_call(
            functools.partial(merge_kernel, parts),
            f"merge{group}",
            [vmem] * parts + [hbm] * len(before),
            [vmem] * 3,
            [half_type, half_type, gain_type],
            [pltpu.VMEM(part_type.shape, part_type.dtype)],
            cost=cost,
        )(me, *prefixes[group], *before)

    def output(group, other, masks, received, out, before, cost=0):
        *out, made = kernel_call(
            functools.partial(output_kernel, dim, owned, half, group * share, masks, other),
            f"output{group}_{other}_{masks[0]}",
            [vmem] * (5 + len(received)) + [hbm] * (len(out) + len(before)),
            [hbm, vmem],
            [pltpu.HBM((1, length, width), jnp.bfloat16), token],
            [
                pltpu.VMEM((len(masks), 2, size, dim), jnp.bfloat16),
                pltpu.VMEM((len(masks), length, STEP * dim), jnp.bfloat16),
                pltpu.SemaphoreType.DMA((len(masks), STEP // 2)),
            ],
            aliases={6 + len(received): 0} if out else {},
            cost=cost,
        )(
            me, queries, in_vmem(inside[group, other][0]), inside[group, other][1],
            in_vmem(gates[group, other]), gains, *received, *out, *before,
        )
        return out, (made,)

    out = ()
    for group in range(GROUPS):
        last = group == GROUPS - 1
        slots = prefixes[group]
        if last:
            out, before = output(group, 0, (0,), slots[:2], out, before)
        *others, came = merge(group, before, 0)
        if group == 0:
            gains = came
        others = [lax.ppermute(other, "core", swap) for other in others]
        before = (came,)
        if last:
            out, before = output(group, 0, (1,), slots[2:], out, before, cost=20)
        else:
            out, before = output(group, 0, (0, 1), slots, out, before)
        out, before = output(group, 1, (0, 1), others, out, before)
    return out[0]


def solution(mesh):
    parts, blocks = mesh.shape["head"], mesh.shape["ctx"]
    names = mesh.axis_names
    at = names.index("ctx")
    shape = mesh.devices.shape[:at] + (blocks // 2, 2) + mesh.devices.shape[at + 1 :]
    finer = Mesh(mesh.devices.reshape(shape), names[:at] + ("z", "core") + names[at + 1 :])
    tokens = P(("z", "core"), "head", None)
    return jax.shard_map(
        functools.partial(on_device, parts, blocks // 2),
        mesh=finer,
        in_specs=(tokens,) * 5 + (P("head"),),
        out_specs=tokens,
        check_vma=False,
    )
```

profile of v0, /device:TPU:0, one launch (start us, length us, event | category | flops | bytes accessed | tf_op | source)
XLA Modules:
  0.0 75.7 jit_solution(1713115334112601494)
XLA Ops:
  0.5 1.4 %pack.1.refs_2_ = f32[8,16,128]{2,1,0:T(8,128)} custom-call(f32[1,16,512]{2,1,0:T(8,128)} %decay_ref.1), custom_call_target="tpu_custom_call" | custom-call | tf_op jit(solution)/shard_map/pack/pallas_call | solution.py:366
  1.9 5.2 %all-to-all-start = ((f32[8,16,128]{2,1,0:T(8,128)}), f32[8,16,128]{2,1,0:T(8,128)S(1)}, u32[]{:S(2)}, u32[]{:S(2)}) async-start(f32[8,16,128]{2,1,0:T(8,128)} %pack.1.refs_2_), calls=%async_computation | async-start | bytes 131072 | tf_op jit(solution)/shard_map/all_to_all | solution.py:371
  8.0 1.8 %load.1 = (bf16[128,2048]{1,0:T(8,128)(2,1)S(1)}, bf16[128,2048]{1,0:T(8,128)(2,1)S(1)}) custom-call(s32[3]{0:T(128)S(1)} %pad_add_fusion.me_ref, bf16[1,128,8192]{2,1,0:T(8,128)(2,1)} %keys_ref.7, bf16[1,128,8192]{2,1,0:T(8,128)(2,1)} %values_ref.7, f32[8,16,128]{2,1,0:T(8,128)S(1)} %copy-done.7), custom_call_target="tpu_custom_call" | custom-call | flops 1 | bytes 1 | tf_op jit(solution)/shard_map/load/pallas_call | solution.py:434
  9.8 2.2 %all-to-all-done.decay_ref = f32[8,16,128]{2,1,0:T(8,128)S(1)} async-done(((f32[8,16,128]{2,1,0:T(8,128)}), f32[8,16,128]{2,1,0:T(8,128)S(1)}, u32[]{:S(2)}, u32[]{:S(2)}) %all-to-all-start) | async-done | bytes 65568 | tf_op jit(solution)/shard_map/all_to_all | solution.py:371
  12.0 2.7 %state0.1 = (bf16[2,528,128]{2,1,0:T(8,128)(2,1)S(1)}, bf16[2,528,128]{2,1,0:T(8,128)(2,1)S(1)}, bf16[2,528,128]{2,1,0:T(8,128)(2,1)S(1)}, bf16[2,528,128]{2,1,0:T(8,128)(2,1)S(1)}) custom-call(s32[3]{0:T(128)S(1)} %pad_add_fusion.me_ref, f32[8,16,128]{2,1,0:T(8,128)S(1)} %all-to-all-done.decay_ref, bf16[128,2048]{1,0:T(8,128)(2,1)S(1)} %get-tuple-element.56.refs_0_, ...), custom_call_target="tpu_custom_call" | custom-call | flops 1 | bytes 1 | tf_op jit(solution)/shard_map/state0/pallas_call | solution.py:446
  16.0 2.2 %collective-permute-start.7 = (bf16[2,528,128]{2,1,0:T(8,128)(2,1)S(1)}, bf16[2,528,128]{2,1,0:T(8,128)(2,1)S(1)}, u32[]{:S(2)}, u32[]{:S(2)}) collective-permute-start(bf16[2,528,128]{2,1,0:T(8,128)(2,1)S(1)} %get-tuple-element.65), channel_id=1, source_target_pairs={{0,24},{8,16},{16,8},{24,0},{1,25},{9,17},{17,9},{25,1},{2,26},{10... | collective-permute-start | bytes 811016 | tf_op jit(solution)/shard_map/ppermute | solution.py:391
  18.2 2.9 %state1.1 = (bf16[2,528,128]{2,1,0:T(8,128)(2,1)S(1)}, bf16[2,528,128]{2,1,0:T(8,128)(2,1)S(1)}, bf16[2,528,128]{2,1,0:T(8,128)(2,1)S(1)}, bf16[2,528,128]{2,1,0:T(8,128)(2,1)S(1)}) custom-call(s32[3]{0:T(128)S(1)} %pad_add_fusion.me_ref, f32[8,16,128]{2,1,0:T(8,128)S(1)} %all-to-all-done.decay_ref, bf16[1,128,8192]{2,1,0:T(8,128)(2,1)} %keys_ref.7, ...), custom_call_target="tpu_custom_call" | custom-call | flops 1 | bytes 1 | tf_op jit(solution)/shard_map/state1/pallas_call | solution.py:446
  21.8 1.3 %collective-permute-start.3 = (bf16[2,528,128]{2,1,0:T(8,128)(2,1)S(1)}, bf16[2,528,128]{2,1,0:T(8,128)(2,1)S(1)}, u32[]{:S(2)}, u32[]{:S(2)}) collective-permute-start(bf16[2,528,128]{2,1,0:T(8,128)(2,1)S(1)} %get-tuple-element.61.rest_0_), channel_id=1, source_target_pairs={{0,16},{8,24},{16,0},{24,8},{1,17},{9,25},{17,1},{25,9},{2,18},{10... | collective-permute-start | bytes 811016 | tf_op jit(solution)/shard_map/ppermute | solution.py:391
  23.1 1.0 %collective-permute-done.5.refs_1_ = bf16[2,528,128]{2,1,0:T(8,128)(2,1)S(1)} collective-permute-done((bf16[2,528,128]{2,1,0:T(8,128)(2,1)S(1)}, bf16[2,528,128]{2,1,0:T(8,128)(2,1)S(1)}, u32[]{:S(2)}, u32[]{:S(2)}) %collective-permute-start.5) | collective-permute-done | bytes 270368 | tf_op jit(solution)/shard_map/ppermute | solution.py:391
  24.8 1.7 %inside0_0.1 = (f32[128,2048]{1,0:T(8,128)S(1)}, f32[2,128,8]{2,1,0:T(8,128)S(1)}, f32[8,128]{1,0:T(8,128)S(1)}) custom-call(s32[3]{0:T(128)S(1)} %pad_add_fusion.me_ref, bf16[1,128,8192]{2,1,0:T(8,128)(2,1)S(1)} %copy-done, bf16[1,128,8192]{2,1,0:T(8,128)(2,1)S(1)} %copy-done.1, bf16[1,128,8192]{2,1,0:T(8,128)(2,1)S(1)} %copy-done.2, ...), custom_call_target="tpu_custom_call" | custom-call | flops 1 | bytes 1 | tf_op jit(solution)/shard_map/inside0_0/pallas_call | solution.py:402
  26.5 1.7 %inside0_1.1 = (f32[128,2048]{1,0:T(8,128)S(1)}, f32[2,128,8]{2,1,0:T(8,128)S(1)}, f32[8,128]{1,0:T(8,128)S(1)}) custom-call(s32[3]{0:T(128)S(1)} %pad_add_fusion.me_ref, bf16[1,128,8192]{2,1,0:T(8,128)(2,1)S(1)} %copy-done, bf16[1,128,8192]{2,1,0:T(8,128)(2,1)S(1)} %copy-done.1, bf16[1,128,8192]{2,1,0:T(8,128)(2,1)S(1)} %copy-done.2, ...), custom_call_target="tpu_custom_call" | custom-call | flops 1 | bytes 1 | tf_op jit(solution)/shard_map/inside0_1/pallas_call | solution.py:402
  28.2 1.8 %collective-permute-done.6.refs_2_ = bf16[2,528,128]{2,1,0:T(8,128)(2,1)S(1)} collective-permute-done((bf16[2,528,128]{2,1,0:T(8,128)(2,1)S(1)}, bf16[2,528,128]{2,1,0:T(8,128)(2,1)S(1)}, u32[]{:S(2)}, u32[]{:S(2)}) %collective-permute-start.6) | collective-permute-done | bytes 270368 | tf_op jit(solution)/shard_map/ppermute | solution.py:391
  30.9 1.6 %collective-permute-start.8 = (bf16[528,128]{1,0:T(8,128)(2,1)S(1)}, bf16[528,128]{1,0:T(8,128)(2,1)S(1)}, u32[]{:S(2)}, u32[]{:S(2)}) collective-permute-start(bf16[528,128]{1,0:T(8,128)(2,1)S(1)} %total0.1.rest_0_.mine_ref), channel_id=1, source_target_pairs={{0,2},{2,0},{4,6},{6,4},{1,3},{3,1},{5,7},{7,5},{8,10},{10,8},{12,... | collective-permute-start | bytes 405512 | tf_op jit(solution)/shard_map/ppermute | solution.py:470
  32.5 1.7 %inside1_0.1 = (f32[128,2048]{1,0:T(8,128)S(1)}, f32[2,128,8]{2,1,0:T(8,128)S(1)}, f32[8,128]{1,0:T(8,128)S(1)}) custom-call(s32[3]{0:T(128)S(1)} %pad_add_fusion.me_ref, bf16[1,128,8192]{2,1,0:T(8,128)(2,1)S(1)} %copy-done, bf16[1,128,8192]{2,1,0:T(8,128)(2,1)S(1)} %copy-done.1, bf16[1,128,8192]{2,1,0:T(8,128)(2,1)S(1)} %copy-done.2, ...), custom_call_target="tpu_custom_call" | custom-call | flops 1 | bytes 1 | tf_op jit(solution)/shard_map/inside1_0/pallas_call | solution.py:402
  34.2 1.7 %collective-permute-done.8.other_ref.refs_4_ = bf16[528,128]{1,0:T(8,128)(2,1)S(1)} collective-permute-done((bf16[528,128]{1,0:T(8,128)(2,1)S(1)}, bf16[528,128]{1,0:T(8,128)(2,1)S(1)}, u32[]{:S(2)}, u32[]{:S(2)}) %collective-permute-start.8) | collective-permute-done | bytes 135200 | tf_op jit(solution)/shard_map/ppermute | solution.py:470
  36.6 2.7 %collective-permute-start.10 = (bf16[528,128]{1,0:T(8,128)(2,1)S(1)}, bf16[528,128]{1,0:T(8,128)(2,1)S(1)}, u32[]{:S(2)}, u32[]{:S(2)}) collective-permute-start(bf16[528,128]{1,0:T(8,128)(2,1)S(1)} %widen0_0.1.refs_0_), channel_id=1, source_target_pairs={{0,4},{2,6},{4,0},{6,2},{1,5},{3,7},{5,1},{7,3},{8,12},{10,14},{12... | collective-permute-start | bytes 405512 | tf_op jit(solution)/shard_map/ppermute | solution.py:470
  39.2 3.1 %gates0.1 = (f32[128,2048]{1,0:T(8,128)}, f32[128,2048]{1,0:T(8,128)}, f32[8,128]{1,0:T(8,128)S(1)}) custom-call(s32[3]{0:T(128)S(1)} %pad_add_fusion.me_ref, bf16[1,128,8192]{2,1,0:T(8,128)(2,1)} %gate_ref.3, bf16[528,128]{1,0:T(8,128)(2,1)S(1)} %widen0_0.1.refs_0_), custom_call_target="tpu_custom_call" | custom-call | flops 1 | bytes 1 | tf_op jit(solution)/shard_map/gates0/pallas_call | solution.py:420
  43.3 1.6 %collective-permute-start.9 = (bf16[528,128]{1,0:T(8,128)(2,1)S(1)}, bf16[528,128]{1,0:T(8,128)(2,1)S(1)}, u32[]{:S(2)}, u32[]{:S(2)}) collective-permute-start(bf16[528,128]{1,0:T(8,128)(2,1)S(1)} %total1.1.refs_6_.mine_ref), channel_id=1, source_target_pairs={{0,2},{2,0},{4,6},{6,4},{1,3},{3,1},{5,7},{7,5},{8,10},{10,8},{12,... | collective-permute-start | bytes 405512 | tf_op jit(solution)/shard_map/ppermute | solution.py:470
  45.9 1.7 %collective-permute-start.11 = (bf16[1040,128]{1,0:T(8,128)(2,1)S(1)}, bf16[1040,128]{1,0:T(8,128)(2,1)S(1)}, u32[]{:S(2)}, u32[]{:S(2)}) collective-permute-start(bf16[1040,128]{1,0:T(8,128)(2,1)S(1)} %get-tuple-element.75), channel_id=1, source_target_pairs={{0,8},{8,0},{16,24},{24,16},{1,9},{9,1},{17,25},{25,17},{2,10},{10... | collective-permute-start | bytes 798728 | tf_op jit(solution)/shard_map/ppermute | solution.py:391
  47.9 1.6 %collective-permute-start.13 = (bf16[1040,128]{1,0:T(8,128)(2,1)S(1)}, bf16[1040,128]{1,0:T(8,128)(2,1)S(1)}, u32[]{:S(2)}, u32[]{:S(2)}) collective-permute-start(bf16[1040,128]{1,0:T(8,128)(2,1)S(1)} %get-tuple-element.77), channel_id=1, source_target_pairs={{0,24},{8,16},{16,8},{24,0},{1,25},{9,17},{17,9},{25,1},{2,26},{10... | collective-permute-start | bytes 798728 | tf_op jit(solution)/shard_map/ppermute | solution.py:391
  50.1 1.2 %collective-permute-start.14 = (bf16[528,128]{1,0:T(8,128)(2,1)S(1)}, bf16[528,128]{1,0:T(8,128)(2,1)S(1)}, u32[]{:S(2)}, u32[]{:S(2)}) collective-permute-start(bf16[528,128]{1,0:T(8,128)(2,1)S(1)} %widen1_0.1.rest_0_), channel_id=1, source_target_pairs={{0,4},{2,6},{4,0},{6,2},{1,5},{3,7},{5,1},{7,3},{8,12},{10,14},{12... | collective-permute-start | bytes 405512 | tf_op jit(solution)/shard_map/ppermute | solution.py:470
  51.2 1.7 %inside1_1.1 = (f32[128,2048]{1,0:T(8,128)S(1)}, f32[2,128,8]{2,1,0:T(8,128)S(1)}, f32[8,128]{1,0:T(8,128)S(1)}) custom-call(s32[3]{0:T(128)S(1)} %pad_add_fusion.me_ref, bf16[1,128,8192]{2,1,0:T(8,128)(2,1)S(1)} %copy-done, bf16[1,128,8192]{2,1,0:T(8,128)(2,1)S(1)} %copy-done.1, bf16[1,128,8192]{2,1,0:T(8,128)(2,1)S(1)} %copy-done.2, ...), custom_call_target="tpu_custom_call" | custom-call | flops 2000000000 | bytes 1 | tf_op jit(solution)/shard_map/inside1_1/pallas_call | solution.py:402
  53.0 3.1 %gates1.1 = (f32[128,2048]{1,0:T(8,128)}, f32[128,2048]{1,0:T(8,128)}, f32[8,128]{1,0:T(8,128)S(1)}) custom-call(s32[3]{0:T(128)S(1)} %pad_add_fusion.me_ref, bf16[1,128,8192]{2,1,0:T(8,128)(2,1)} %gate_ref.3, f32[8,128]{1,0:T(8,128)S(1)} %get-tuple-element.73.refs_0_), custom_call_target="tpu_custom_call" | custom-call | flops 1 | bytes 1 | tf_op jit(solution)/shard_map/gates1/pallas_call | solution.py:420
  56.1 1.4 %collective-permute-done.14.refs_5_ = bf16[528,128]{1,0:T(8,128)(2,1)S(1)} collective-permute-done((bf16[528,128]{1,0:T(8,128)(2,1)S(1)}, bf16[528,128]{1,0:T(8,128)(2,1)S(1)}, u32[]{:S(2)}, u32[]{:S(2)}) %collective-permute-start.14) | collective-permute-done | bytes 135200 | tf_op jit(solution)/shard_map/ppermute | solution.py:470
  58.4 1.8 %collective-permute-start.15 = (bf16[1040,128]{1,0:T(8,128)(2,1)S(1)}, bf16[1040,128]{1,0:T(8,128)(2,1)S(1)}, u32[]{:S(2)}, u32[]{:S(2)}) collective-permute-start(bf16[1040,128]{1,0:T(8,128)(2,1)S(1)} %get-tuple-element.81), channel_id=1, source_target_pairs={{0,8},{8,0},{16,24},{24,16},{1,9},{9,1},{17,25},{25,17},{2,10},{10... | collective-permute-start | bytes 798728 | tf_op jit(solution)/shard_map/ppermute | solution.py:391
  60.4 1.6 %collective-permute-start.17 = (bf16[1040,128]{1,0:T(8,128)(2,1)S(1)}, bf16[1040,128]{1,0:T(8,128)(2,1)S(1)}, u32[]{:S(2)}, u32[]{:S(2)}) collective-permute-start(bf16[1040,128]{1,0:T(8,128)(2,1)S(1)} %get-tuple-element.83), channel_id=1, source_target_pairs={{0,24},{8,16},{16,8},{24,0},{1,25},{9,17},{17,9},{25,1},{2,26},{10... | collective-permute-start | bytes 798728 | tf_op jit(solution)/shard_map/ppermute | solution.py:391
  63.2 2.1 %output0_0_0.1 = (bf16[1,128,8192]{2,1,0:T(8,128)(2,1)}, f32[8,128]{1,0:T(8,128)S(1)}) custom-call(s32[3]{0:T(128)S(1)} %pad_add_fusion.me_ref, bf16[1,128,8192]{2,1,0:T(8,128)(2,1)S(1)} %copy-done, f32[128,2048]{1,0:T(8,128)S(1)} %get-tuple-element.92.inside_ref, f32[2,128,8]{2,1,0:T(8,128)S(1)} %get-tuple-element.93.down_ref, f32[128,2048]{1,0:T(8,128)S(1)} %copy-done.6, ...), custom_call_target="tpu_custom_call" | custom-call | flops 1 | bytes 1 | tf_op jit(solution)/shard_map/output0_0_0/pallas_call | solution.py:540
  65.3 2.0 %output0_1_0.1 = (bf16[1,128,8192]{2,1,0:T(8,128)(2,1)}, f32[8,128]{1,0:T(8,128)S(1)}) custom-call(s32[3]{0:T(128)S(1)} %pad_add_fusion.me_ref, bf16[1,128,8192]{2,1,0:T(8,128)(2,1)S(1)} %copy-done, f32[128,2048]{1,0:T(8,128)S(1)} %get-tuple-element.87.inside_ref, f32[2,128,8]{2,1,0:T(8,128)S(1)} %get-tuple-element.88.down_ref, ...), custom_call_target="tpu_custom_call", output_to_operand_aliasing={{0}: (8, {})} | custom-call | flops 1 | bytes 1 | tf_op jit(solution)/shard_map/output0_1_0/pallas_call | solution.py:540
  67.3 1.7 %output1_0_0.1 = (bf16[1,128,8192]{2,1,0:T(8,128)(2,1)}, f32[8,128]{1,0:T(8,128)S(1)}) custom-call(s32[3]{0:T(128)S(1)} %pad_add_fusion.me_ref, bf16[1,128,8192]{2,1,0:T(8,128)(2,1)S(1)} %copy-done, f32[128,2048]{1,0:T(8,128)S(1)} %get-tuple-element.84.inside_ref, f32[2,128,8]{2,1,0:T(8,128)S(1)} %get-tuple-element.85.down_ref, ...), custom_call_target="tpu_custom_call", output_to_operand_aliasing={{0}: (8, {})} | custom-call | flops 1 | bytes 1 | tf_op jit(solution)/shard_map/output1_0_0/pallas_call | solution.py:540
  69.0 1.1 %collective-permute-done.16.refs_2_.refs_0_ = bf16[1040,128]{1,0:T(8,128)(2,1)S(1)} collective-permute-done((bf16[1040,128]{1,0:T(8,128)(2,1)S(1)}, bf16[1040,128]{1,0:T(8,128)(2,1)S(1)}, u32[]{:S(2)}, u32[]{:S(2)}) %collective-permute-start.16) | collective-permute-done | bytes 266272 | tf_op jit(solution)/shard_map/ppermute | solution.py:391
  71.4 1.7 %output1_0_1.1 = (bf16[1,128,8192]{2,1,0:T(8,128)(2,1)}, f32[8,128]{1,0:T(8,128)S(1)}) custom-call(s32[3]{0:T(128)S(1)} %pad_add_fusion.me_ref, bf16[1,128,8192]{2,1,0:T(8,128)(2,1)S(1)} %copy-done, f32[128,2048]{1,0:T(8,128)S(1)} %get-tuple-element.84.inside_ref, f32[2,128,8]{2,1,0:T(8,128)S(1)} %get-tuple-element.85.down_ref, ...), custom_call_target="tpu_custom_call", output_to_operand_aliasing={{0}: (8, {})} | custom-call | flops 20000000000 | bytes 1 | tf_op jit(solution)/shard_map/output1_0_1/pallas_call | solution.py:540
  73.1 2.6 %output1_1_0.1 = (bf16[1,128,8192]{2,1,0:T(8,128)(2,1)}, f32[8,128]{1,0:T(8,128)}) custom-call(s32[3]{0:T(128)S(1)} %pad_add_fusion.me_ref, bf16[1,128,8192]{2,1,0:T(8,128)(2,1)S(1)} %copy-done, f32[128,2048]{1,0:T(8,128)S(1)} %get-tuple-element.71.inside_ref, f32[2,128,8]{2,1,0:T(8,128)S(1)} %get-tuple-element.72.down_ref, ...), custom_call_target="tpu_custom_call", output_to_operand_aliasing={{0}: (8, {})} | custom-call | flops 1 | bytes 1 | tf_op jit(solution)/shard_map/output1_1_0/pallas_call | solution.py:540
  (56 shorter events, 11.9 us)
Async XLA Ops:
  0.0 12.0 %collective-permute-start = (bf16[1,128,8192]{2,1,0:T(8,128)(2,1)}, bf16[1,128,8192]{2,1,0:T(8,128)(2,1)S(1)}, u32[]{:S(2)}, u32[]{:S(2)}) collective-permute-start(bf16[1,128,8192]{2,1,0:T(8,128)(2,1)} %keys_ref.7), channel_id=1, source_target_pairs={{0,1},{1,0},{2,3},{3,2},{4,5},{5,4},{6,7},{7,6},{8,9},{9,8},{10,11... | collective-permute-start | bytes 6291464 | tf_op jit(solution)/shard_map/ppermute | solution.py:365
  0.5 11.6 %collective-permute-start.1 = (bf16[1,128,8192]{2,1,0:T(8,128)(2,1)}, bf16[1,128,8192]{2,1,0:T(8,128)(2,1)}, u32[]{:S(2)}, u32[]{:S(2)}) collective-permute-start(bf16[1,128,8192]{2,1,0:T(8,128)(2,1)} %values_ref.7), channel_id=1, source_target_pairs={{0,1},{1,0},{2,3},{3,2},{4,5},{5,4},{6,7},{7,6},{8,9},{9,8},{10,11... | collective-permute-start | bytes 6291464 | tf_op jit(solution)/shard_map/ppermute | solution.py:364
  1.9 10.1 %all-to-all-start = ((f32[8,16,128]{2,1,0:T(8,128)}), f32[8,16,128]{2,1,0:T(8,128)S(1)}, u32[]{:S(2)}, u32[]{:S(2)}) async-start(f32[8,16,128]{2,1,0:T(8,128)} %pack.1.refs_2_), calls=%async_computation | async-start | bytes 131072 | tf_op jit(solution)/shard_map/all_to_all | solution.py:371
  7.1 0.8 %copy-start.7 = (f32[8,16,128]{2,1,0:T(8,128)S(1)}, f32[8,16,128]{2,1,0:T(8,128)}, u32[]{:S(2)}) copy-start(f32[8,16,128]{2,1,0:T(8,128)} %pack.1.refs_2_) | copy-start | bytes 196612
  14.7 9.4 %collective-permute-start.5 = (bf16[2,528,128]{2,1,0:T(8,128)(2,1)S(1)}, bf16[2,528,128]{2,1,0:T(8,128)(2,1)S(1)}, u32[]{:S(2)}, u32[]{:S(2)}) collective-permute-start(bf16[2,528,128]{2,1,0:T(8,128)(2,1)S(1)} %get-tuple-element.64), channel_id=1, source_target_pairs={{0,8},{8,0},{16,24},{24,16},{1,9},{9,1},{17,25},{25,17},{2,10},{10... | collective-permute-start | bytes 811016 | tf_op jit(solution)/shard_map/ppermute | solution.py:391
  15.3 14.7 %collective-permute-start.6 = (bf16[2,528,128]{2,1,0:T(8,128)(2,1)S(1)}, bf16[2,528,128]{2,1,0:T(8,128)(2,1)S(1)}, u32[]{:S(2)}, u32[]{:S(2)}) collective-permute-start(bf16[2,528,128]{2,1,0:T(8,128)(2,1)S(1)} %get-tuple-element.58.refs_4_), channel_id=1, source_target_pairs={{0,16},{8,24},{16,0},{24,8},{1,17},{9,25},{17,1},{25,9},{2,18},{10... | collective-permute-start | bytes 811016 | tf_op jit(solution)/shard_map/ppermute | solution.py:391
  16.0 8.8 %copy-start = (bf16[1,128,8192]{2,1,0:T(8,128)(2,1)S(1)}, bf16[1,128,8192]{2,1,0:T(8,128)(2,1)}, u32[]{:S(2)}) copy-start(bf16[1,128,8192]{2,1,0:T(8,128)(2,1)} %queries_ref.17) | copy-start | bytes 6291460
  16.0 8.8 %copy-start.1 = (bf16[1,128,8192]{2,1,0:T(8,128)(2,1)S(1)}, bf16[1,128,8192]{2,1,0:T(8,128)(2,1)}, u32[]{:S(2)}) copy-start(bf16[1,128,8192]{2,1,0:T(8,128)(2,1)} %keys_ref.7) | copy-start | bytes 6291460
  16.0 8.8 %copy-start.2 = (bf16[1,128,8192]{2,1,0:T(8,128)(2,1)S(1)}, bf16[1,128,8192]{2,1,0:T(8,128)(2,1)}, u32[]{:S(2)}) copy-start(bf16[1,128,8192]{2,1,0:T(8,128)(2,1)} %values_ref.7) | copy-start | bytes 6291460
  16.0 14.0 %collective-permute-start.7 = (bf16[2,528,128]{2,1,0:T(8,128)(2,1)S(1)}, bf16[2,528,128]{2,1,0:T(8,128)(2,1)S(1)}, u32[]{:S(2)}, u32[]{:S(2)}) collective-permute-start(bf16[2,528,128]{2,1,0:T(8,128)(2,1)S(1)} %get-tuple-element.65), channel_id=1, source_target_pairs={{0,24},{8,16},{16,8},{24,0},{1,25},{9,17},{17,9},{25,1},{2,26},{10... | collective-permute-start | bytes 811016 | tf_op jit(solution)/shard_map/ppermute | solution.py:391
  21.2 21.2 %collective-permute-start.2 = (bf16[2,528,128]{2,1,0:T(8,128)(2,1)S(1)}, bf16[2,528,128]{2,1,0:T(8,128)(2,1)S(1)}, u32[]{:S(2)}, u32[]{:S(2)}) collective-permute-start(bf16[2,528,128]{2,1,0:T(8,128)(2,1)S(1)} %get-tuple-element.60), channel_id=1, source_target_pairs={{0,8},{8,0},{16,24},{24,16},{1,9},{9,1},{17,25},{25,17},{2,10},{10... | collective-permute-start | bytes 811016 | tf_op jit(solution)/shard_map/ppermute | solution.py:391
  21.8 20.6 %collective-permute-start.3 = (bf16[2,528,128]{2,1,0:T(8,128)(2,1)S(1)}, bf16[2,528,128]{2,1,0:T(8,128)(2,1)S(1)}, u32[]{:S(2)}, u32[]{:S(2)}) collective-permute-start(bf16[2,528,128]{2,1,0:T(8,128)(2,1)S(1)} %get-tuple-element.61.rest_0_), channel_id=1, source_target_pairs={{0,16},{8,24},{16,0},{24,8},{1,17},{9,25},{17,1},{25,9},{2,18},{10... | collective-permute-start | bytes 811016 | tf_op jit(solution)/shard_map/ppermute | solution.py:391
  24.1 18.3 %collective-permute-start.4 = (bf16[2,528,128]{2,1,0:T(8,128)(2,1)S(1)}, bf16[2,528,128]{2,1,0:T(8,128)(2,1)S(1)}, u32[]{:S(2)}, u32[]{:S(2)}) collective-permute-start(bf16[2,528,128]{2,1,0:T(8,128)(2,1)S(1)} %get-tuple-element.62), channel_id=1, source_target_pairs={{0,24},{8,16},{16,8},{24,0},{1,25},{9,17},{17,9},{25,1},{2,26},{10... | collective-permute-start | bytes 811016 | tf_op jit(solution)/shard_map/ppermute | solution.py:391
  30.9 5.1 %collective-permute-start.8 = (bf16[528,128]{1,0:T(8,128)(2,1)S(1)}, bf16[528,128]{1,0:T(8,128)(2,1)S(1)}, u32[]{:S(2)}, u32[]{:S(2)}) collective-permute-start(bf16[528,128]{1,0:T(8,128)(2,1)S(1)} %total0.1.rest_0_.mine_ref), channel_id=1, source_target_pairs={{0,2},{2,0},{4,6},{6,4},{1,3},{3,1},{5,7},{7,5},{8,10},{10,8},{12,... | collective-permute-start | bytes 405512 | tf_op jit(solution)/shard_map/ppermute | solution.py:470
  34.2 10.7 %copy-start.8 = (bf16[2048]{0:T(1024)(128)(2,1)S(1)}, bf16[2048]{0:T(1024)(128)(2,1)}, u32[]{:S(2)}) copy-start(bf16[2048]{0:T(1024)(128)(2,1)} %param.11) | copy-start | bytes 12292
  36.6 8.3 %collective-permute-start.10 = (bf16[528,128]{1,0:T(8,128)(2,1)S(1)}, bf16[528,128]{1,0:T(8,128)(2,1)S(1)}, u32[]{:S(2)}, u32[]{:S(2)}) collective-permute-start(bf16[528,128]{1,0:T(8,128)(2,1)S(1)} %widen0_0.1.refs_0_), channel_id=1, source_target_pairs={{0,4},{2,6},{4,0},{6,2},{1,5},{3,7},{5,1},{7,3},{8,12},{10,14},{12... | collective-permute-start | bytes 405512 | tf_op jit(solution)/shard_map/ppermute | solution.py:470
  43.3 6.2 %collective-permute-start.9 = (bf16[528,128]{1,0:T(8,128)(2,1)S(1)}, bf16[528,128]{1,0:T(8,128)(2,1)S(1)}, u32[]{:S(2)}, u32[]{:S(2)}) collective-permute-start(bf16[528,128]{1,0:T(8,128)(2,1)S(1)} %total1.1.refs_6_.mine_ref), channel_id=1, source_target_pairs={{0,2},{2,0},{4,6},{6,4},{1,3},{3,1},{5,7},{7,5},{8,10},{10,8},{12,... | collective-permute-start | bytes 405512 | tf_op jit(solution)/shard_map/ppermute | solution.py:470
  45.9 14.5 %collective-permute-start.11 = (bf16[1040,128]{1,0:T(8,128)(2,1)S(1)}, bf16[1040,128]{1,0:T(8,128)(2,1)S(1)}, u32[]{:S(2)}, u32[]{:S(2)}) collective-permute-start(bf16[1040,128]{1,0:T(8,128)(2,1)S(1)} %get-tuple-element.75), channel_id=1, source_target_pairs={{0,8},{8,0},{16,24},{24,16},{1,9},{9,1},{17,25},{25,17},{2,10},{10... | collective-permute-start | bytes 798728 | tf_op jit(solution)/shard_map/ppermute | solution.py:391
  47.6 14.3 %collective-permute-start.12 = (bf16[1040,128]{1,0:T(8,128)(2,1)S(1)}, bf16[1040,128]{1,0:T(8,128)(2,1)S(1)}, u32[]{:S(2)}, u32[]{:S(2)}) collective-permute-start(bf16[1040,128]{1,0:T(8,128)(2,1)S(1)} %get-tuple-element.76), channel_id=1, source_target_pairs={{0,16},{8,24},{16,0},{24,8},{1,17},{9,25},{17,1},{25,9},{2,18},{10... | collective-permute-start | bytes 798728 | tf_op jit(solution)/shard_map/ppermute | solution.py:391
  47.9 14.1 %collective-permute-start.13 = (bf16[1040,128]{1,0:T(8,128)(2,1)S(1)}, bf16[1040,128]{1,0:T(8,128)(2,1)S(1)}, u32[]{:S(2)}, u32[]{:S(2)}) collective-permute-start(bf16[1040,128]{1,0:T(8,128)(2,1)S(1)} %get-tuple-element.77), channel_id=1, source_target_pairs={{0,24},{8,16},{16,8},{24,0},{1,25},{9,17},{17,9},{25,1},{2,26},{10... | collective-permute-start | bytes 798728 | tf_op jit(solution)/shard_map/ppermute | solution.py:391
  50.1 7.3 %collective-permute-start.14 = (bf16[528,128]{1,0:T(8,128)(2,1)S(1)}, bf16[528,128]{1,0:T(8,128)(2,1)S(1)}, u32[]{:S(2)}, u32[]{:S(2)}) collective-permute-start(bf16[528,128]{1,0:T(8,128)(2,1)S(1)} %widen1_0.1.rest_0_), channel_id=1, source_target_pairs={{0,4},{2,6},{4,0},{6,2},{1,5},{3,7},{5,1},{7,3},{8,12},{10,14},{12... | collective-permute-start | bytes 405512 | tf_op jit(solution)/shard_map/ppermute | solution.py:470
  52.9 10.2 %copy-start.6 = (f32[128,2048]{1,0:T(8,128)S(1)}, f32[128,2048]{1,0:T(8,128)}, u32[]{:S(2)}) copy-start(f32[128,2048]{1,0:T(8,128)} %get-tuple-element.94.gate_ref) | copy-start | bytes 3145732
  58.4 8.9 %collective-permute-start.15 = (bf16[1040,128]{1,0:T(8,128)(2,1)S(1)}, bf16[1040,128]{1,0:T(8,128)(2,1)S(1)}, u32[]{:S(2)}, u32[]{:S(2)}) collective-permute-start(bf16[1040,128]{1,0:T(8,128)(2,1)S(1)} %get-tuple-element.81), channel_id=1, source_target_pairs={{0,8},{8,0},{16,24},{24,16},{1,9},{9,1},{17,25},{25,17},{2,10},{10... | collective-permute-start | bytes 798728 | tf_op jit(solution)/shard_map/ppermute | solution.py:391
  60.2 9.9 %collective-permute-start.16 = (bf16[1040,128]{1,0:T(8,128)(2,1)S(1)}, bf16[1040,128]{1,0:T(8,128)(2,1)S(1)}, u32[]{:S(2)}, u32[]{:S(2)}) collective-permute-start(bf16[1040,128]{1,0:T(8,128)(2,1)S(1)} %get-tuple-element.82), channel_id=1, source_target_pairs={{0,16},{8,24},{16,0},{24,8},{1,17},{9,25},{17,1},{25,9},{2,18},{10... | collective-permute-start | bytes 798728 | tf_op jit(solution)/shard_map/ppermute | solution.py:391
  60.4 9.8 %collective-permute-start.17 = (bf16[1040,128]{1,0:T(8,128)(2,1)S(1)}, bf16[1040,128]{1,0:T(8,128)(2,1)S(1)}, u32[]{:S(2)}, u32[]{:S(2)}) collective-permute-start(bf16[1040,128]{1,0:T(8,128)(2,1)S(1)} %get-tuple-element.83), channel_id=1, source_target_pairs={{0,24},{8,16},{16,8},{24,0},{1,25},{9,17},{17,9},{25,1},{2,26},{10... | collective-permute-start | bytes 798728 | tf_op jit(solution)/shard_map/ppermute | solution.py:391
  62.6 2.7 %collective-permute-start.18 = (bf16[2,512,128]{2,1,0:T(8,128)(2,1)S(1)}, bf16[2,512,128]{2,1,0:T(8,128)(2,1)S(1)}, u32[]{:S(2)}, u32[]{:S(2)}) collective-permute-start(bf16[2,512,128]{2,1,0:T(8,128)(2,1)S(1)} %get-tuple-element.90), channel_id=1, source_target_pairs={{0,1},{1,0},{2,3},{3,2},{4,5},{5,4},{6,7},{7,6},{8,9},{9,8},{10,11... | collective-permute-start | bytes 786440 | tf_op jit(solution)/shard_map/ppermute | solution.py:568
  62.7 2.6 %collective-permute-start.19 = (bf16[2,512,128]{2,1,0:T(8,128)(2,1)S(1)}, bf16[2,512,128]{2,1,0:T(8,128)(2,1)S(1)}, u32[]{:S(2)}, u32[]{:S(2)}) collective-permute-start(bf16[2,512,128]{2,1,0:T(8,128)(2,1)S(1)} %get-tuple-element.91), channel_id=1, source_target_pairs={{0,1},{1,0},{2,3},{3,2},{4,5},{5,4},{6,7},{7,6},{8,9},{9,8},{10,11... | collective-permute-start | bytes 786440 | tf_op jit(solution)/shard_map/ppermute | solution.py:568
  63.2 2.1 %copy-start.4 = (f32[128,2048]{1,0:T(8,128)S(1)}, f32[128,2048]{1,0:T(8,128)}, u32[]{:S(2)}) copy-start(f32[128,2048]{1,0:T(8,128)} %get-tuple-element.89.gate_ref) | copy-start | bytes 3145732
  65.3 2.0 %copy-start.5 = (f32[128,2048]{1,0:T(8,128)S(1)}, f32[128,2048]{1,0:T(8,128)}, u32[]{:S(2)}) copy-start(f32[128,2048]{1,0:T(8,128)} %get-tuple-element.86.gate_ref) | copy-start | bytes 3145732
  70.8 2.3 %collective-permute-start.20 = (bf16[2,512,128]{2,1,0:T(8,128)(2,1)S(1)}, bf16[2,512,128]{2,1,0:T(8,128)(2,1)S(1)}, u32[]{:S(2)}, u32[]{:S(2)}) collective-permute-start(bf16[2,512,128]{2,1,0:T(8,128)(2,1)S(1)} %get-tuple-element.100), channel_id=1, source_target_pairs={{0,1},{1,0},{2,3},{3,2},{4,5},{5,4},{6,7},{7,6},{8,9},{9,8},{10,11... | collective-permute-start | bytes 786440 | tf_op jit(solution)/shard_map/ppermute | solution.py:568
  70.9 2.2 %collective-permute-start.21 = (bf16[2,512,128]{2,1,0:T(8,128)(2,1)S(1)}, bf16[2,512,128]{2,1,0:T(8,128)(2,1)S(1)}, u32[]{:S(2)}, u32[]{:S(2)}) collective-permute-start(bf16[2,512,128]{2,1,0:T(8,128)(2,1)S(1)} %get-tuple-element.101), channel_id=1, source_target_pairs={{0,1},{1,0},{2,3},{3,2},{4,5},{5,4},{6,7},{7,6},{8,9},{9,8},{10,11... | collective-permute-start | bytes 786440 | tf_op jit(solution)/shard_map/ppermute | solution.py:568
  71.4 1.7 %copy-start.3 = (f32[128,2048]{1,0:T(8,128)S(1)}, f32[128,2048]{1,0:T(8,128)}, u32[]{:S(2)}) copy-start(f32[128,2048]{1,0:T(8,128)} %get-tuple-element.74.gate_ref) | copy-start | bytes 3145732
where the time goes:
time: 76.1 us; the launch traced here: 75.7 us
  Pallas kernels  37.9 us (50%)
  starting transfers between devices  27.2 us (36%)
  waiting for transfers between devices  9.35 us (12%)
  local copies, waits for them, and re-layouts  0.88 us (1%)
    ppermute x12, starting transfers between devices, exchange(): arrived[slot] = lax.ppermute(slots[slot], 'head', pairs)  13.3 us
    pallas_call x5, Pallas kernels, output(): kernel_call(functools.partial(output_kernel, dim, owned, half, group * sh...  10 us
    ppermute x4, starting transfers between devices, with_plane(): return lax.ppermute(total, 'z', pairs)  7.09 us
    pallas_call x4, Pallas kernels, inside_part(): kernel_call(functools.partial(inside_kernel, dim, half, group * share, sh...  6.74 us
    pallas_call x2, Pallas kernels, gates_of(): kernel_call(functools.partial(gate_kernel, half, group * share, share, di...  6.23 us
    pallas_call x2, Pallas kernels, on_device(): kernel_call(functools.partial(state_kernel, dim, owned, half, group * sha...  5.56 us
    all_to_all x1, starting transfers between devices, on_device(): decay = lax.all_to_all(packed, ('core', 'head'), 0, 0, tiled=True)  5.17 us
    ppermute x12, waiting for transfers between devices, exchange(): arrived[slot] = lax.ppermute(slots[slot], 'head', pairs)  3.99 us
  transfers between devices with their start and end apart: 23, of which 6 were waited for; matrix products, arithmetic and copies ran while one was open for 0% of the time, Pallas kernels for 42%

commit v1 on v0

--- a/solution.py
+++ b/solution.py
@@ -56,28 +56,6 @@
     for place in range(packed_ref.shape[0]):
         start = place % parts * length
         packed_ref[place] = decay_ref[0, :, start : start + length]
-
-
-def gate_kernel(half, begin, share, dim, me_ref, gate_ref, *refs):
-    *results, done_ref, copy_ref, result_ref, done = refs[-6:]
-    width = share * dim
-    loads, stores = [], []
-    for at, out_ref in enumerate(results):
-        first = (me_ref[1] if at == 0 else 1 - me_ref[1]) * half + begin
-        columns = pl.ds(pl.multiple_of(first * dim, width), width)
-        loads.append(pltpu.make_async_copy(gate_ref.at[0, :, columns], copy_ref.at[at], done.at[at]))
-        stores.append(pltpu.make_async_copy(result_ref.at[at], out_ref, done.at[2 + at]))
-        loads[-1].start()
-    for at in range(len(results)):
-        loads[at].wait()
-        for head in range(share):
-            c = slice(head * dim, (head + 1) * dim)
-            turned = jnp.tanh(0.5 * copy_ref[at, :, c].astype(jnp.float32))
-            result_ref[at, :, c] = 0.5 + 0.5 * turned
-        stores[at].start()
-    done_ref[...] = jnp.zeros_like(done_ref)
-    for store in stores:
-        store.wait()
 
 
 def heads_at(first, head, dim):
@@ -155,9 +133,10 @@
 
 
 def inside_kernel(
-    dim, half, begin, count, other, me_ref, queries_ref, keys_ref, values_ref, decay_ref, *rest
+    dim, half, begin, count, other, me_ref,
+    queries_ref, keys_ref, values_ref, gate_ref, decay_ref, *rest,
 ):
-    inside_ref, down_ref, done_ref = rest[-3:]
+    inside_ref, down_ref, sigmoid_ref, done_ref = rest[-4:]
     core = me_ref[1]
     length = decay_ref.shape[2]
     rows = lax.broadcasted_iota(jnp.int32, (length, length), 0)
@@ -178,6 +157,8 @@
         for head, c in enumerate(columns):
             at = (turn * STEP + head) * dim
             inside_ref[:, at : at + dim] = dot(weights[head], values_ref[0, :, c], NN)
+            turned = jnp.tanh(0.5 * gate_ref[0, :, c].astype(jnp.float32))
+            sigmoid_ref[:, at : at + dim] = 0.5 + 0.5 * turned
     done_ref[...] = jnp.zeros_like(done_ref)
 
 
@@ -382,7 +363,7 @@
 
     own = in_hbm(keys), in_hbm(values)
     share = half // GROUPS
-    keys, values, queries = (in_vmem(array) for array in (keys, values, queries))
+    keys, values, queries, gate = (in_vmem(array) for array in (keys, values, queries, gate))
 
     def exchange(slots):
         arrived = list(slots)
@@ -402,33 +383,16 @@
         *inside[group, other], made = kernel_call(
             functools.partial(inside_kernel, dim, half, group * share, share, other),
             f"inside{group}_{other}",
-            [vmem] * 4 + [hbm] * len(before),
-            [vmem] * 3,
+            [vmem] * 5 + [hbm] * len(before),
+            [vmem] * 4,
             [
                 pltpu.VMEM((length, share * dim), jnp.float32),
                 jax.ShapeDtypeStruct((share // STEP, length, STEP), jnp.float32),
+                pltpu.VMEM((length, share * dim), jnp.float32),
                 token,
             ],
             cost=cost,
-        )(me, queries, keys, values, decay, *before)
-        return (made,)
-
-    gate_type = jax.ShapeDtypeStruct((length, share * dim), jnp.float32)
-    gates = {}
-
-    def gates_of(group, before):
-        gates[group, 0], gates[group, 1], made = kernel_call(
-            functools.partial(gate_kernel, half, group * share, share, dim),
-            f"gates{group}",
-            [hbm] * (1 + len(before)),
-            [hbm, hbm, vmem],
-            [pltpu.HBM(gate_type.shape, gate_type.dtype)] * 2 + [token],
-            [
-                pltpu.VMEM((2, length, share * dim), jnp.bfloat16),
-                pltpu.VMEM((2,) + gate_type.shape, jnp.float32),
-                pltpu.SemaphoreType.DMA((4,)),
-            ],
-        )(me, in_hbm(gate), *before)
+        )(me, queries, keys, values, gate, decay, *before)
         return (made,)
 
     first_slices = kernel_call(
@@ -516,7 +480,6 @@
             stretches.append(with_plane(total, step))
         while group == GROUPS - 1 and len(inside) < 2 * GROUPS:
             before = inside_part(before, 2)
-        before = gates_of(group, before)
     prefix = prefix_of(GROUPS - 1, before)
     before = tuple(prefix[:1])
     prefixes.append(exchange(prefix))
@@ -552,7 +515,7 @@
             cost=cost,
         )(
             me, queries, in_vmem(inside[group, other][0]), inside[group, other][1],
-            in_vmem(gates[group, other]), gains, *received, *out, *before,
+            in_vmem(inside[group, other][2]), gains, *received, *out, *before,
         )
         return out, (made,)
 

time: 76.1 us -> 75.9 us (level)
  Pallas kernels: 37.9 us -> 31.9 us
  waiting for transfers between devices: 9.35 us -> 14.4 us
  starting transfers between devices: 27.2 us -> 28.1 us
    pallas_call x2 -> x0, Pallas kernels: 6.23 us -> none  [gates_of(): kernel_call(functools.partial(gate_kernel, half, group * share, share, di...]
    ppermute x4, waiting for transfers between devices: 3.09 us -> 6.12 us  [with_plane(): return lax.ppermute(total, 'z', pairs)]
    ppermute x12, waiting for transfers between devices: 3.99 us -> 6.02 us  [exchange(): arrived[slot] = lax.ppermute(slots[slot], 'head', pairs)]
    ppermute x4, starting transfers between devices: 7.09 us -> 7.88 us  [with_plane(): return lax.ppermute(total, 'z', pairs)]
  transfers between devices with their start and end apart: 23 -> 23, of which waited for: 6 -> 9; matrix products, arithmetic and copies ran while one was open for 0% -> 0% of each run, Pallas kernels for 42% -> 34%
where the time goes in v1:
time: 75.9 us; the launch traced here: 75.6 us
  Pallas kernels  31.9 us (42%)
  starting transfers between devices  28.1 us (37%)
  waiting for transfers between devices  14.4 us (19%)
  local copies, waits for them, and re-layouts  0.86 us (1%)
    ppermute x12, starting transfers between devices, exchange(): arrived[slot] = lax.ppermute(slots[slot], 'head', pairs)  13.4 us
    pallas_call x5, Pallas kernels, output(): kernel_call(functools.partial(output_kernel, dim, owned, half, group * sh...  10 us
    ppermute x4, starting transfers between devices, with_plane(): return lax.ppermute(total, 'z', pairs)  7.88 us
    pallas_call x4, Pallas kernels, inside_part(): kernel_call(functools.partial(inside_kernel, dim, half, group * share, sh...  7.02 us
    ppermute x4, waiting for transfers between devices, with_plane(): return lax.ppermute(total, 'z', pairs)  6.12 us
    ppermute x12, waiting for transfers between devices, exchange(): arrived[slot] = lax.ppermute(slots[slot], 'head', pairs)  6.02 us
    pallas_call x2, Pallas kernels, on_device(): kernel_call(functools.partial(state_kernel, dim, owned, half, group * sha...  5.57 us
    all_to_all x1, starting transfers between devices, on_device(): decay = lax.all_to_all(packed, ('core', 'head'), 0, 0, tiled=True)  5.17 us
  transfers between devices with their start and end apart: 23, of which 9 were waited for; matrix products, arithmetic and copies ran while one was open for 0% of the time, Pallas kernels for 34%

profile of v1, /device:TPU:0, one launch (start us, length us, event | category | flops | bytes accessed | tf_op | source)
XLA Modules:
  0.0 75.6 jit_solution(17228153860658545356)
XLA Ops:
  0.5 1.4 %pack.1.refs_2_ = f32[8,16,128]{2,1,0:T(8,128)} custom-call(f32[1,16,512]{2,1,0:T(8,128)} %decay_ref.1), custom_call_target="tpu_custom_call" | custom-call | tf_op jit(solution)/shard_map/pack/pallas_call | solution.py:347
  1.9 5.2 %all-to-all-start = ((f32[8,16,128]{2,1,0:T(8,128)}), f32[8,16,128]{2,1,0:T(8,128)S(1)}, u32[]{:S(2)}, u32[]{:S(2)}) async-start(f32[8,16,128]{2,1,0:T(8,128)} %pack.1.refs_2_), calls=%async_computation | async-start | bytes 131072 | tf_op jit(solution)/shard_map/all_to_all | solution.py:352
  8.0 1.8 %load.1 = (bf16[128,2048]{1,0:T(8,128)(2,1)S(1)}, bf16[128,2048]{1,0:T(8,128)(2,1)S(1)}) custom-call(s32[3]{0:T(128)S(1)} %pad_add_fusion.me_ref, bf16[1,128,8192]{2,1,0:T(8,128)(2,1)} %keys_ref.7, bf16[1,128,8192]{2,1,0:T(8,128)(2,1)} %values_ref.7, f32[8,16,128]{2,1,0:T(8,128)S(1)} %copy-done.4), custom_call_target="tpu_custom_call" | custom-call | flops 1 | bytes 1 | tf_op jit(solution)/shard_map/load/pallas_call | solution.py:398
  9.8 2.2 %all-to-all-done.decay_ref = f32[8,16,128]{2,1,0:T(8,128)S(1)} async-done(((f32[8,16,128]{2,1,0:T(8,128)}), f32[8,16,128]{2,1,0:T(8,128)S(1)}, u32[]{:S(2)}, u32[]{:S(2)}) %all-to-all-start) | async-done | bytes 65568 | tf_op jit(solution)/shard_map/all_to_all | solution.py:352
  12.0 2.7 %state0.1 = (bf16[2,528,128]{2,1,0:T(8,128)(2,1)S(1)}, bf16[2,528,128]{2,1,0:T(8,128)(2,1)S(1)}, bf16[2,528,128]{2,1,0:T(8,128)(2,1)S(1)}, bf16[2,528,128]{2,1,0:T(8,128)(2,1)S(1)}) custom-call(s32[3]{0:T(128)S(1)} %pad_add_fusion.me_ref, f32[8,16,128]{2,1,0:T(8,128)S(1)} %all-to-all-done.decay_ref, bf16[128,2048]{1,0:T(8,128)(2,1)S(1)} %get-tuple-element.54.refs_0_, ...), custom_call_target="tpu_custom_call" | custom-call | flops 1 | bytes 1 | tf_op jit(solution)/shard_map/state0/pallas_call | solution.py:410
  16.0 2.3 %collective-permute-start.7 = (bf16[2,528,128]{2,1,0:T(8,128)(2,1)S(1)}, bf16[2,528,128]{2,1,0:T(8,128)(2,1)S(1)}, u32[]{:S(2)}, u32[]{:S(2)}) collective-permute-start(bf16[2,528,128]{2,1,0:T(8,128)(2,1)S(1)} %get-tuple-element.63), channel_id=1, source_target_pairs={{0,24},{8,16},{16,8},{24,0},{1,25},{9,17},{17,9},{25,1},{2,26},{10... | collective-permute-start | bytes 811016 | tf_op jit(solution)/shard_map/ppermute | solution.py:372
  18.3 2.9 %state1.1 = (bf16[2,528,128]{2,1,0:T(8,128)(2,1)S(1)}, bf16[2,528,128]{2,1,0:T(8,128)(2,1)S(1)}, bf16[2,528,128]{2,1,0:T(8,128)(2,1)S(1)}, bf16[2,528,128]{2,1,0:T(8,128)(2,1)S(1)}) custom-call(s32[3]{0:T(128)S(1)} %pad_add_fusion.me_ref, f32[8,16,128]{2,1,0:T(8,128)S(1)} %all-to-all-done.decay_ref, bf16[1,128,8192]{2,1,0:T(8,128)(2,1)} %keys_ref.7, ...), custom_call_target="tpu_custom_call" | custom-call | flops 1 | bytes 1 | tf_op jit(solution)/shard_map/state1/pallas_call | solution.py:410
  21.2 1.1 %collective-permute-start.2 = (bf16[2,528,128]{2,1,0:T(8,128)(2,1)S(1)}, bf16[2,528,128]{2,1,0:T(8,128)(2,1)S(1)}, u32[]{:S(2)}, u32[]{:S(2)}) collective-permute-start(bf16[2,528,128]{2,1,0:T(8,128)(2,1)S(1)} %get-tuple-element.58), channel_id=1, source_target_pairs={{0,8},{8,0},{16,24},{24,16},{1,9},{9,1},{17,25},{25,17},{2,10},{10... | collective-permute-start | bytes 811016 | tf_op jit(solution)/shard_map/ppermute | solution.py:372
  24.8 1.8 %inside0_0.1 = (f32[128,2048]{1,0:T(8,128)S(1)}, f32[2,128,8]{2,1,0:T(8,128)S(1)}, f32[128,2048]{1,0:T(8,128)S(1)}, f32[8,128]{1,0:T(8,128)S(1)}) custom-call(s32[3]{0:T(128)S(1)} %pad_add_fusion.me_ref, bf16[1,128,8192]{2,1,0:T(8,128)(2,1)S(1)} %copy-done, bf16[1,128,8192]{2,1,0:T(8,128)(2,1)S(1)} %copy-done.1, bf16[1,128,8192]{2,1,0:T(8,128)(2,1)S(1)} %copy-done.2, ...), custom_call_target="tpu_custom_call" | custom-call | flops 1 | bytes 1 | tf_op jit(solution)/shard_map/inside0_0/pallas_call | solution.py:383
  26.6 1.8 %inside0_1.1 = (f32[128,2048]{1,0:T(8,128)S(1)}, f32[2,128,8]{2,1,0:T(8,128)S(1)}, f32[128,2048]{1,0:T(8,128)S(1)}, f32[8,128]{1,0:T(8,128)S(1)}) custom-call(s32[3]{0:T(128)S(1)} %pad_add_fusion.me_ref, bf16[1,128,8192]{2,1,0:T(8,128)(2,1)S(1)} %copy-done, bf16[1,128,8192]{2,1,0:T(8,128)(2,1)S(1)} %copy-done.1, bf16[1,128,8192]{2,1,0:T(8,128)(2,1)S(1)} %copy-done.2, ...), custom_call_target="tpu_custom_call" | custom-call | flops 1 | bytes 1 | tf_op jit(solution)/shard_map/inside0_1/pallas_call | solution.py:383
  28.3 1.1 %collective-permute-done.6.refs_2_ = bf16[2,528,128]{2,1,0:T(8,128)(2,1)S(1)} collective-permute-done((bf16[2,528,128]{2,1,0:T(8,128)(2,1)S(1)}, bf16[2,528,128]{2,1,0:T(8,128)(2,1)S(1)}, u32[]{:S(2)}, u32[]{:S(2)}) %collective-permute-start.6) | collective-permute-done | bytes 270368 | tf_op jit(solution)/shard_map/ppermute | solution.py:372
  30.9 1.6 %collective-permute-start.8 = (bf16[528,128]{1,0:T(8,128)(2,1)S(1)}, bf16[528,128]{1,0:T(8,128)(2,1)S(1)}, u32[]{:S(2)}, u32[]{:S(2)}) collective-permute-start(bf16[528,128]{1,0:T(8,128)(2,1)S(1)} %total0.1.rest_0_.mine_ref), channel_id=1, source_target_pairs={{0,2},{2,0},{4,6},{6,4},{1,3},{3,1},{5,7},{7,5},{8,10},{10,8},{12,... | collective-permute-start | bytes 405512 | tf_op jit(solution)/shard_map/ppermute | solution.py:434
  32.5 1.8 %inside1_0.1 = (f32[128,2048]{1,0:T(8,128)S(1)}, f32[2,128,8]{2,1,0:T(8,128)S(1)}, f32[128,2048]{1,0:T(8,128)S(1)}, f32[8,128]{1,0:T(8,128)S(1)}) custom-call(s32[3]{0:T(128)S(1)} %pad_add_fusion.me_ref, bf16[1,128,8192]{2,1,0:T(8,128)(2,1)S(1)} %copy-done, bf16[1,128,8192]{2,1,0:T(8,128)(2,1)S(1)} %copy-done.1, bf16[1,128,8192]{2,1,0:T(8,128)(2,1)S(1)} %copy-done.2, ...), custom_call_target="tpu_custom_call" | custom-call | flops 1 | bytes 1 | tf_op jit(solution)/shard_map/inside1_0/pallas_call | solution.py:383
  34.3 1.7 %collective-permute-done.8.other_ref.refs_4_ = bf16[528,128]{1,0:T(8,128)(2,1)S(1)} collective-permute-done((bf16[528,128]{1,0:T(8,128)(2,1)S(1)}, bf16[528,128]{1,0:T(8,128)(2,1)S(1)}, u32[]{:S(2)}, u32[]{:S(2)}) %collective-permute-start.8) | collective-permute-done | bytes 135200 | tf_op jit(solution)/shard_map/ppermute | solution.py:434
  36.6 2.7 %collective-permute-start.10 = (bf16[528,128]{1,0:T(8,128)(2,1)S(1)}, bf16[528,128]{1,0:T(8,128)(2,1)S(1)}, u32[]{:S(2)}, u32[]{:S(2)}) collective-permute-start(bf16[528,128]{1,0:T(8,128)(2,1)S(1)} %widen0_0.1.refs_4_), channel_id=1, source_target_pairs={{0,4},{2,6},{4,0},{6,2},{1,5},{3,7},{5,1},{7,3},{8,12},{10,14},{12... | collective-permute-start | bytes 405512 | tf_op jit(solution)/shard_map/ppermute | solution.py:434
  39.3 1.6 %collective-permute-done.3.refs_2_ = bf16[2,528,128]{2,1,0:T(8,128)(2,1)S(1)} collective-permute-done((bf16[2,528,128]{2,1,0:T(8,128)(2,1)S(1)}, bf16[2,528,128]{2,1,0:T(8,128)(2,1)S(1)}, u32[]{:S(2)}, u32[]{:S(2)}) %collective-permute-start.3) | collective-permute-done | bytes 270368 | tf_op jit(solution)/shard_map/ppermute | solution.py:372
  41.8 1.6 %collective-permute-start.9 = (bf16[528,128]{1,0:T(8,128)(2,1)S(1)}, bf16[528,128]{1,0:T(8,128)(2,1)S(1)}, u32[]{:S(2)}, u32[]{:S(2)}) collective-permute-start(bf16[528,128]{1,0:T(8,128)(2,1)S(1)} %total1.1.refs_6_.mine_ref), channel_id=1, source_target_pairs={{0,2},{2,0},{4,6},{6,4},{1,3},{3,1},{5,7},{7,5},{8,10},{10,8},{12,... | collective-permute-start | bytes 405512 | tf_op jit(solution)/shard_map/ppermute | solution.py:434
  44.1 1.0 %prefix0.1 = (bf16[1040,128]{1,0:T(8,128)(2,1)S(1)}, bf16[1040,128]{1,0:T(8,128)(2,1)S(1)}, bf16[1040,128]{1,0:T(8,128)(2,1)S(1)}, bf16[1040,128]{1,0:T(8,128)(2,1)S(1)}) custom-call(s32[3]{0:T(128)S(1)} %pad_add_fusion.me_ref, bf16[16,128]{1,0:T(8,128)(2,1)S(1)} %bitcast.4, bf16[2,528,128]{2,1,0:T(8,128)(2,1)S(1)} %get-tuple-element.61.refs_0_, ...), custom_call_target="tpu_custom_call" | custom-call | flops 1 | bytes 1 | tf_op jit(solution)/shard_map/prefix0/pallas_call | solution.py:447
  45.1 1.7 %collective-permute-start.11 = (bf16[1040,128]{1,0:T(8,128)(2,1)S(1)}, bf16[1040,128]{1,0:T(8,128)(2,1)S(1)}, u32[]{:S(2)}, u32[]{:S(2)}) collective-permute-start(bf16[1040,128]{1,0:T(8,128)(2,1)S(1)} %get-tuple-element.71), channel_id=1, source_target_pairs={{0,8},{8,0},{16,24},{24,16},{1,9},{9,1},{17,25},{25,17},{2,10},{10... | collective-permute-start | bytes 798728 | tf_op jit(solution)/shard_map/ppermute | solution.py:372
  47.1 1.6 %collective-permute-start.13 = (bf16[1040,128]{1,0:T(8,128)(2,1)S(1)}, bf16[1040,128]{1,0:T(8,128)(2,1)S(1)}, u32[]{:S(2)}, u32[]{:S(2)}) collective-permute-start(bf16[1040,128]{1,0:T(8,128)(2,1)S(1)} %get-tuple-element.73), channel_id=1, source_target_pairs={{0,24},{8,16},{16,8},{24,0},{1,25},{9,17},{17,9},{25,1},{2,26},{10... | collective-permute-start | bytes 798728 | tf_op jit(solution)/shard_map/ppermute | solution.py:372
  49.3 1.9 %collective-permute-start.14 = (bf16[528,128]{1,0:T(8,128)(2,1)S(1)}, bf16[528,128]{1,0:T(8,128)(2,1)S(1)}, u32[]{:S(2)}, u32[]{:S(2)}) collective-permute-start(bf16[528,128]{1,0:T(8,128)(2,1)S(1)} %widen1_0.1.rest_0_), channel_id=1, source_target_pairs={{0,4},{2,6},{4,0},{6,2},{1,5},{3,7},{5,1},{7,3},{8,12},{10,14},{12... | collective-permute-start | bytes 405512 | tf_op jit(solution)/shard_map/ppermute | solution.py:434
  51.2 1.7 %inside1_1.1 = (f32[128,2048]{1,0:T(8,128)S(1)}, f32[2,128,8]{2,1,0:T(8,128)S(1)}, f32[128,2048]{1,0:T(8,128)S(1)}, f32[8,128]{1,0:T(8,128)S(1)}) custom-call(s32[3]{0:T(128)S(1)} %pad_add_fusion.me_ref, bf16[1,128,8192]{2,1,0:T(8,128)(2,1)S(1)} %copy-done, bf16[1,128,8192]{2,1,0:T(8,128)(2,1)S(1)} %copy-done.1, bf16[1,128,8192]{2,1,0:T(8,128)(2,1)S(1)} %copy-done.2, ...), custom_call_target="tpu_custom_call" | custom-call | flops 2000000000 | bytes 1 | tf_op jit(solution)/shard_map/inside1_1/pallas_call | solution.py:383
  53.0 3.7 %collective-permute-done.14.refs_5_ = bf16[528,128]{1,0:T(8,128)(2,1)S(1)} collective-permute-done((bf16[528,128]{1,0:T(8,128)(2,1)S(1)}, bf16[528,128]{1,0:T(8,128)(2,1)S(1)}, u32[]{:S(2)}, u32[]{:S(2)}) %collective-permute-start.14) | collective-permute-done | bytes 135200 | tf_op jit(solution)/shard_map/ppermute | solution.py:434
  56.7 1.0 %prefix1.1 = (bf16[1040,128]{1,0:T(8,128)(2,1)S(1)}, bf16[1040,128]{1,0:T(8,128)(2,1)S(1)}, bf16[1040,128]{1,0:T(8,128)(2,1)S(1)}, bf16[1040,128]{1,0:T(8,128)(2,1)S(1)}) custom-call(s32[3]{0:T(128)S(1)} %pad_add_fusion.me_ref, bf16[16,128]{1,0:T(8,128)(2,1)S(1)} %bitcast.5, bf16[2,528,128]{2,1,0:T(8,128)(2,1)S(1)} %get-tuple-element.57.refs_0_, ...), custom_call_target="tpu_custom_call" | custom-call | flops 1 | bytes 1 | tf_op jit(solution)/shard_map/prefix1/pallas_call | solution.py:447
  57.7 1.7 %collective-permute-start.15 = (bf16[1040,128]{1,0:T(8,128)(2,1)S(1)}, bf16[1040,128]{1,0:T(8,128)(2,1)S(1)}, u32[]{:S(2)}, u32[]{:S(2)}) collective-permute-start(bf16[1040,128]{1,0:T(8,128)(2,1)S(1)} %get-tuple-element.77), channel_id=1, source_target_pairs={{0,8},{8,0},{16,24},{24,16},{1,9},{9,1},{17,25},{25,17},{2,10},{10... | collective-permute-start | bytes 798728 | tf_op jit(solution)/shard_map/ppermute | solution.py:372
  59.7 1.6 %collective-permute-start.17 = (bf16[1040,128]{1,0:T(8,128)(2,1)S(1)}, bf16[1040,128]{1,0:T(8,128)(2,1)S(1)}, u32[]{:S(2)}, u32[]{:S(2)}) collective-permute-start(bf16[1040,128]{1,0:T(8,128)(2,1)S(1)} %get-tuple-element.79), channel_id=1, source_target_pairs={{0,24},{8,16},{16,8},{24,0},{1,25},{9,17},{17,9},{25,1},{2,26},{10... | collective-permute-start | bytes 798728 | tf_op jit(solution)/shard_map/ppermute | solution.py:372
  62.5 2.1 %output0_0_0.1 = (bf16[1,128,8192]{2,1,0:T(8,128)(2,1)}, f32[8,128]{1,0:T(8,128)S(1)}) custom-call(s32[3]{0:T(128)S(1)} %pad_add_fusion.me_ref, bf16[1,128,8192]{2,1,0:T(8,128)(2,1)S(1)} %copy-done, f32[128,2048]{1,0:T(8,128)S(1)} %get-tuple-element.88.inside_ref, f32[2,128,8]{2,1,0:T(8,128)S(1)} %get-tuple-element.89.down_ref, ...), custom_call_target="tpu_custom_call" | custom-call | flops 1 | bytes 1 | tf_op jit(solution)/shard_map/output0_0_0/pallas_call | solution.py:503
  64.6 2.0 %output0_1_0.1 = (bf16[1,128,8192]{2,1,0:T(8,128)(2,1)}, f32[8,128]{1,0:T(8,128)S(1)}) custom-call(s32[3]{0:T(128)S(1)} %pad_add_fusion.me_ref, bf16[1,128,8192]{2,1,0:T(8,128)(2,1)S(1)} %copy-done, f32[128,2048]{1,0:T(8,128)S(1)} %get-tuple-element.83.inside_ref, f32[2,128,8]{2,1,0:T(8,128)S(1)} %get-tuple-element.84.down_ref, ...), custom_call_target="tpu_custom_call", output_to_operand_aliasing={{0}: (8, {})} | custom-call | flops 1 | bytes 1 | tf_op jit(solution)/shard_map/output0_1_0/pallas_call | solution.py:503
  66.6 1.7 %output1_0_0.1 = (bf16[1,128,8192]{2,1,0:T(8,128)(2,1)}, f32[8,128]{1,0:T(8,128)S(1)}) custom-call(s32[3]{0:T(128)S(1)} %pad_add_fusion.me_ref, bf16[1,128,8192]{2,1,0:T(8,128)(2,1)S(1)} %copy-done, f32[128,2048]{1,0:T(8,128)S(1)} %get-tuple-element.80.inside_ref, f32[2,128,8]{2,1,0:T(8,128)S(1)} %get-tuple-element.81.down_ref, ...), custom_call_target="tpu_custom_call", output_to_operand_aliasing={{0}: (8, {})} | custom-call | flops 1 | bytes 1 | tf_op jit(solution)/shard_map/output1_0_0/pallas_call | solution.py:503
  68.3 1.7 %collective-permute-done.16.refs_2_.refs_0_ = bf16[1040,128]{1,0:T(8,128)(2,1)S(1)} collective-permute-done((bf16[1040,128]{1,0:T(8,128)(2,1)S(1)}, bf16[1040,128]{1,0:T(8,128)(2,1)S(1)}, u32[]{:S(2)}, u32[]{:S(2)}) %collective-permute-start.16) | collective-permute-done | bytes 266272 | tf_op jit(solution)/shard_map/ppermute | solution.py:372
  71.3 1.7 %output1_0_1.1 = (bf16[1,128,8192]{2,1,0:T(8,128)(2,1)}, f32[8,128]{1,0:T(8,128)S(1)}) custom-call(s32[3]{0:T(128)S(1)} %pad_add_fusion.me_ref, bf16[1,128,8192]{2,1,0:T(8,128)(2,1)S(1)} %copy-done, f32[128,2048]{1,0:T(8,128)S(1)} %get-tuple-element.80.inside_ref, f32[2,128,8]{2,1,0:T(8,128)S(1)} %get-tuple-element.81.down_ref, ...), custom_call_target="tpu_custom_call", output_to_operand_aliasing={{0}: (8, {})} | custom-call | flops 20000000000 | bytes 1 | tf_op jit(solution)/shard_map/output1_0_1/pallas_call | solution.py:503
  73.0 2.6 %output1_1_0.1 = (bf16[1,128,8192]{2,1,0:T(8,128)(2,1)}, f32[8,128]{1,0:T(8,128)}) custom-call(s32[3]{0:T(128)S(1)} %pad_add_fusion.me_ref, bf16[1,128,8192]{2,1,0:T(8,128)(2,1)S(1)} %copy-done, f32[128,2048]{1,0:T(8,128)S(1)} %get-tuple-element.68.inside_ref, f32[2,128,8]{2,1,0:T(8,128)S(1)} %get-tuple-element.69.down_ref, ...), custom_call_target="tpu_custom_call", output_to_operand_aliasing={{0}: (8, {})} | custom-call | flops 1 | bytes 1 | tf_op jit(solution)/shard_map/output1_1_0/pallas_call | solution.py:503
  (48 shorter events, 12.6 us)
Async XLA Ops:
  0.0 12.0 %collective-permute-start = (bf16[1,128,8192]{2,1,0:T(8,128)(2,1)}, bf16[1,128,8192]{2,1,0:T(8,128)(2,1)S(1)}, u32[]{:S(2)}, u32[]{:S(2)}) collective-permute-start(bf16[1,128,8192]{2,1,0:T(8,128)(2,1)} %keys_ref.7), channel_id=1, source_target_pairs={{0,1},{1,0},{2,3},{3,2},{4,5},{5,4},{6,7},{7,6},{8,9},{9,8},{10,11... | collective-permute-start | bytes 6291464 | tf_op jit(solution)/shard_map/ppermute | solution.py:346
  0.5 11.6 %collective-permute-start.1 = (bf16[1,128,8192]{2,1,0:T(8,128)(2,1)}, bf16[1,128,8192]{2,1,0:T(8,128)(2,1)}, u32[]{:S(2)}, u32[]{:S(2)}) collective-permute-start(bf16[1,128,8192]{2,1,0:T(8,128)(2,1)} %values_ref.7), channel_id=1, source_target_pairs={{0,1},{1,0},{2,3},{3,2},{4,5},{5,4},{6,7},{7,6},{8,9},{9,8},{10,11... | collective-permute-start | bytes 6291464 | tf_op jit(solution)/shard_map/ppermute | solution.py:345
  1.9 10.1 %all-to-all-start = ((f32[8,16,128]{2,1,0:T(8,128)}), f32[8,16,128]{2,1,0:T(8,128)S(1)}, u32[]{:S(2)}, u32[]{:S(2)}) async-start(f32[8,16,128]{2,1,0:T(8,128)} %pack.1.refs_2_), calls=%async_computation | async-start | bytes 131072 | tf_op jit(solution)/shard_map/all_to_all | solution.py:352
  7.1 0.8 %copy-start.4 = (f32[8,16,128]{2,1,0:T(8,128)S(1)}, f32[8,16,128]{2,1,0:T(8,128)}, u32[]{:S(2)}) copy-start(f32[8,16,128]{2,1,0:T(8,128)} %pack.1.refs_2_) | copy-start | bytes 196612
  14.7 9.4 %collective-permute-start.5 = (bf16[2,528,128]{2,1,0:T(8,128)(2,1)S(1)}, bf16[2,528,128]{2,1,0:T(8,128)(2,1)S(1)}, u32[]{:S(2)}, u32[]{:S(2)}) collective-permute-start(bf16[2,528,128]{2,1,0:T(8,128)(2,1)S(1)} %get-tuple-element.62), channel_id=1, source_target_pairs={{0,8},{8,0},{16,24},{24,16},{1,9},{9,1},{17,25},{25,17},{2,10},{10... | collective-permute-start | bytes 811016 | tf_op jit(solution)/shard_map/ppermute | solution.py:372
  15.3 14.1 %collective-permute-start.6 = (bf16[2,528,128]{2,1,0:T(8,128)(2,1)S(1)}, bf16[2,528,128]{2,1,0:T(8,128)(2,1)S(1)}, u32[]{:S(2)}, u32[]{:S(2)}) collective-permute-start(bf16[2,528,128]{2,1,0:T(8,128)(2,1)S(1)} %get-tuple-element.56.refs_4_), channel_id=1, source_target_pairs={{0,16},{8,24},{16,0},{24,8},{1,17},{9,25},{17,1},{25,9},{2,18},{10... | collective-permute-start | bytes 811016 | tf_op jit(solution)/shard_map/ppermute | solution.py:372
  16.0 8.8 %copy-start = (bf16[1,128,8192]{2,1,0:T(8,128)(2,1)S(1)}, bf16[1,128,8192]{2,1,0:T(8,128)(2,1)}, u32[]{:S(2)}) copy-start(bf16[1,128,8192]{2,1,0:T(8,128)(2,1)} %queries_ref.17) | copy-start | bytes 6291460
  16.0 8.8 %copy-start.1 = (bf16[1,128,8192]{2,1,0:T(8,128)(2,1)S(1)}, bf16[1,128,8192]{2,1,0:T(8,128)(2,1)}, u32[]{:S(2)}) copy-start(bf16[1,128,8192]{2,1,0:T(8,128)(2,1)} %keys_ref.7) | copy-start | bytes 6291460
  16.0 8.8 %copy-start.2 = (bf16[1,128,8192]{2,1,0:T(8,128)(2,1)S(1)}, bf16[1,128,8192]{2,1,0:T(8,128)(2,1)}, u32[]{:S(2)}) copy-start(bf16[1,128,8192]{2,1,0:T(8,128)(2,1)} %values_ref.7) | copy-start | bytes 6291460
  16.0 8.8 %copy-start.3 = (bf16[1,128,8192]{2,1,0:T(8,128)(2,1)S(1)}, bf16[1,128,8192]{2,1,0:T(8,128)(2,1)}, u32[]{:S(2)}) copy-start(bf16[1,128,8192]{2,1,0:T(8,128)(2,1)} %gate_ref.7) | copy-start | bytes 6291460
  16.0 14.0 %collective-permute-start.7 = (bf16[2,528,128]{2,1,0:T(8,128)(2,1)S(1)}, bf16[2,528,128]{2,1,0:T(8,128)(2,1)S(1)}, u32[]{:S(2)}, u32[]{:S(2)}) collective-permute-start(bf16[2,528,128]{2,1,0:T(8,128)(2,1)S(1)} %get-tuple-element.63), channel_id=1, source_target_pairs={{0,24},{8,16},{16,8},{24,0},{1,25},{9,17},{17,9},{25,1},{2,26},{10... | collective-permute-start | bytes 811016 | tf_op jit(solution)/shard_map/ppermute | solution.py:372
  21.2 18.0 %collective-permute-start.2 = (bf16[2,528,128]{2,1,0:T(8,128)(2,1)S(1)}, bf16[2,528,128]{2,1,0:T(8,128)(2,1)S(1)}, u32[]{:S(2)}, u32[]{:S(2)}) collective-permute-start(bf16[2,528,128]{2,1,0:T(8,128)(2,1)S(1)} %get-tuple-element.58), channel_id=1, source_target_pairs={{0,8},{8,0},{16,24},{24,16},{1,9},{9,1},{17,25},{25,17},{2,10},{10... | collective-permute-start | bytes 811016 | tf_op jit(solution)/shard_map/ppermute | solution.py:372
  22.3 18.6 %collective-permute-start.3 = (bf16[2,528,128]{2,1,0:T(8,128)(2,1)S(1)}, bf16[2,528,128]{2,1,0:T(8,128)(2,1)S(1)}, u32[]{:S(2)}, u32[]{:S(2)}) collective-permute-start(bf16[2,528,128]{2,1,0:T(8,128)(2,1)S(1)} %get-tuple-element.59.rest_0_), channel_id=1, source_target_pairs={{0,16},{8,24},{16,0},{24,8},{1,17},{9,25},{17,1},{25,9},{2,18},{10... | collective-permute-start | bytes 811016 | tf_op jit(solution)/shard_map/ppermute | solution.py:372
  24.1 16.8 %collective-permute-start.4 = (bf16[2,528,128]{2,1,0:T(8,128)(2,1)S(1)}, bf16[2,528,128]{2,1,0:T(8,128)(2,1)S(1)}, u32[]{:S(2)}, u32[]{:S(2)}) collective-permute-start(bf16[2,528,128]{2,1,0:T(8,128)(2,1)S(1)} %get-tuple-element.60), channel_id=1, source_target_pairs={{0,24},{8,16},{16,8},{24,0},{1,25},{9,17},{17,9},{25,1},{2,26},{10... | collective-permute-start | bytes 811016 | tf_op jit(solution)/shard_map/ppermute | solution.py:372
  30.9 13.3 %copy-start.5 = (bf16[2048]{0:T(1024)(128)(2,1)S(1)}, bf16[2048]{0:T(1024)(128)(2,1)}, u32[]{:S(2)}) copy-start(bf16[2048]{0:T(1024)(128)(2,1)} %param.11) | copy-start | bytes 12292
  30.9 5.1 %collective-permute-start.8 = (bf16[528,128]{1,0:T(8,128)(2,1)S(1)}, bf16[528,128]{1,0:T(8,128)(2,1)S(1)}, u32[]{:S(2)}, u32[]{:S(2)}) collective-permute-start(bf16[528,128]{1,0:T(8,128)(2,1)S(1)} %total0.1.rest_0_.mine_ref), channel_id=1, source_target_pairs={{0,2},{2,0},{4,6},{6,4},{1,3},{3,1},{5,7},{7,5},{8,10},{10,8},{12,... | collective-permute-start | bytes 405512 | tf_op jit(solution)/shard_map/ppermute | solution.py:434
  36.6 7.5 %collective-permute-start.10 = (bf16[528,128]{1,0:T(8,128)(2,1)S(1)}, bf16[528,128]{1,0:T(8,128)(2,1)S(1)}, u32[]{:S(2)}, u32[]{:S(2)}) collective-permute-start(bf16[528,128]{1,0:T(8,128)(2,1)S(1)} %widen0_0.1.refs_4_), channel_id=1, source_target_pairs={{0,4},{2,6},{4,0},{6,2},{1,5},{3,7},{5,1},{7,3},{8,12},{10,14},{12... | collective-permute-start | bytes 405512 | tf_op jit(solution)/shard_map/ppermute | solution.py:434
  41.8 6.9 %collective-permute-start.9 = (bf16[528,128]{1,0:T(8,128)(2,1)S(1)}, bf16[528,128]{1,0:T(8,128)(2,1)S(1)}, u32[]{:S(2)}, u32[]{:S(2)}) collective-permute-start(bf16[528,128]{1,0:T(8,128)(2,1)S(1)} %total1.1.refs_6_.mine_ref), channel_id=1, source_target_pairs={{0,2},{2,0},{4,6},{6,4},{1,3},{3,1},{5,7},{7,5},{8,10},{10,8},{12,... | collective-permute-start | bytes 405512 | tf_op jit(solution)/shard_map/ppermute | solution.py:434
  45.1 14.6 %collective-permute-start.11 = (bf16[1040,128]{1,0:T(8,128)(2,1)S(1)}, bf16[1040,128]{1,0:T(8,128)(2,1)S(1)}, u32[]{:S(2)}, u32[]{:S(2)}) collective-permute-start(bf16[1040,128]{1,0:T(8,128)(2,1)S(1)} %get-tuple-element.71), channel_id=1, source_target_pairs={{0,8},{8,0},{16,24},{24,16},{1,9},{9,1},{17,25},{25,17},{2,10},{10... | collective-permute-start | bytes 798728 | tf_op jit(solution)/shard_map/ppermute | solution.py:372
  46.8 14.5 %collective-permute-start.12 = (bf16[1040,128]{1,0:T(8,128)(2,1)S(1)}, bf16[1040,128]{1,0:T(8,128)(2,1)S(1)}, u32[]{:S(2)}, u32[]{:S(2)}) collective-permute-start(bf16[1040,128]{1,0:T(8,128)(2,1)S(1)} %get-tuple-element.72), channel_id=1, source_target_pairs={{0,16},{8,24},{16,0},{24,8},{1,17},{9,25},{17,1},{25,9},{2,18},{10... | collective-permute-start | bytes 798728 | tf_op jit(solution)/shard_map/ppermute | solution.py:372
  47.1 14.2 %collective-permute-start.13 = (bf16[1040,128]{1,0:T(8,128)(2,1)S(1)}, bf16[1040,128]{1,0:T(8,128)(2,1)S(1)}, u32[]{:S(2)}, u32[]{:S(2)}) collective-permute-start(bf16[1040,128]{1,0:T(8,128)(2,1)S(1)} %get-tuple-element.73), channel_id=1, source_target_pairs={{0,24},{8,16},{16,8},{24,0},{1,25},{9,17},{17,9},{25,1},{2,26},{10... | collective-permute-start | bytes 798728 | tf_op jit(solution)/shard_map/ppermute | solution.py:372
  49.3 7.4 %collective-permute-start.14 = (bf16[528,128]{1,0:T(8,128)(2,1)S(1)}, bf16[528,128]{1,0:T(8,128)(2,1)S(1)}, u32[]{:S(2)}, u32[]{:S(2)}) collective-permute-start(bf16[528,128]{1,0:T(8,128)(2,1)S(1)} %widen1_0.1.rest_0_), channel_id=1, source_target_pairs={{0,4},{2,6},{4,0},{6,2},{1,5},{3,7},{5,1},{7,3},{8,12},{10,14},{12... | collective-permute-start | bytes 405512 | tf_op jit(solution)/shard_map/ppermute | solution.py:434
  57.7 8.9 %collective-permute-start.15 = (bf16[1040,128]{1,0:T(8,128)(2,1)S(1)}, bf16[1040,128]{1,0:T(8,128)(2,1)S(1)}, u32[]{:S(2)}, u32[]{:S(2)}) collective-permute-start(bf16[1040,128]{1,0:T(8,128)(2,1)S(1)} %get-tuple-element.77), channel_id=1, source_target_pairs={{0,8},{8,0},{16,24},{24,16},{1,9},{9,1},{17,25},{25,17},{2,10},{10... | collective-permute-start | bytes 798728 | tf_op jit(solution)/shard_map/ppermute | solution.py:372
  59.4 10.7 %collective-permute-start.16 = (bf16[1040,128]{1,0:T(8,128)(2,1)S(1)}, bf16[1040,128]{1,0:T(8,128)(2,1)S(1)}, u32[]{:S(2)}, u32[]{:S(2)}) collective-permute-start(bf16[1040,128]{1,0:T(8,128)(2,1)S(1)} %get-tuple-element.78), channel_id=1, source_target_pairs={{0,16},{8,24},{16,0},{24,8},{1,17},{9,25},{17,1},{25,9},{2,18},{10... | collective-permute-start | bytes 798728 | tf_op jit(solution)/shard_map/ppermute | solution.py:372
  59.7 10.4 %collective-permute-start.17 = (bf16[1040,128]{1,0:T(8,128)(2,1)S(1)}, bf16[1040,128]{1,0:T(8,128)(2,1)S(1)}, u32[]{:S(2)}, u32[]{:S(2)}) collective-permute-start(bf16[1040,128]{1,0:T(8,128)(2,1)S(1)} %get-tuple-element.79), channel_id=1, source_target_pairs={{0,24},{8,16},{16,8},{24,0},{1,25},{9,17},{17,9},{25,1},{2,26},{10... | collective-permute-start | bytes 798728 | tf_op jit(solution)/shard_map/ppermute | solution.py:372
  61.9 2.7 %collective-permute-start.18 = (bf16[2,512,128]{2,1,0:T(8,128)(2,1)S(1)}, bf16[2,512,128]{2,1,0:T(8,128)(2,1)S(1)}, u32[]{:S(2)}, u32[]{:S(2)}) collective-permute-start(bf16[2,512,128]{2,1,0:T(8,128)(2,1)S(1)} %get-tuple-element.86), channel_id=1, source_target_pairs={{0,1},{1,0},{2,3},{3,2},{4,5},{5,4},{6,7},{7,6},{8,9},{9,8},{10,11... | collective-permute-start | bytes 786440 | tf_op jit(solution)/shard_map/ppermute | solution.py:531
  62.0 2.6 %collective-permute-start.19 = (bf16[2,512,128]{2,1,0:T(8,128)(2,1)S(1)}, bf16[2,512,128]{2,1,0:T(8,128)(2,1)S(1)}, u32[]{:S(2)}, u32[]{:S(2)}) collective-permute-start(bf16[2,512,128]{2,1,0:T(8,128)(2,1)S(1)} %get-tuple-element.87), channel_id=1, source_target_pairs={{0,1},{1,0},{2,3},{3,2},{4,5},{5,4},{6,7},{7,6},{8,9},{9,8},{10,11... | collective-permute-start | bytes 786440 | tf_op jit(solution)/shard_map/ppermute | solution.py:531
  70.7 2.3 %collective-permute-start.20 = (bf16[2,512,128]{2,1,0:T(8,128)(2,1)S(1)}, bf16[2,512,128]{2,1,0:T(8,128)(2,1)S(1)}, u32[]{:S(2)}, u32[]{:S(2)}) collective-permute-start(bf16[2,512,128]{2,1,0:T(8,128)(2,1)S(1)} %get-tuple-element.96), channel_id=1, source_target_pairs={{0,1},{1,0},{2,3},{3,2},{4,5},{5,4},{6,7},{7,6},{8,9},{9,8},{10,11... | collective-permute-start | bytes 786440 | tf_op jit(solution)/shard_map/ppermute | solution.py:531
  70.8 2.2 %collective-permute-start.21 = (bf16[2,512,128]{2,1,0:T(8,128)(2,1)S(1)}, bf16[2,512,128]{2,1,0:T(8,128)(2,1)S(1)}, u32[]{:S(2)}, u32[]{:S(2)}) collective-permute-start(bf16[2,512,128]{2,1,0:T(8,128)(2,1)S(1)} %get-tuple-element.97), channel_id=1, source_target_pairs={{0,1},{1,0},{2,3},{3,2},{4,5},{5,4},{6,7},{7,6},{8,9},{9,8},{10,11... | collective-permute-start | bytes 786440 | tf_op jit(solution)/shard_map/ppermute | solution.py:531

commit v2 on v1

--- a/solution.py
+++ b/solution.py
@@ -236,13 +236,13 @@
             result_ref[2 * size :, :] = gain_ref[...]
 
 
-def merge_kernel(parts, me_ref, *refs):
+def merge_kernel(parts, order, me_ref, *refs):
     slots, gain_ref, prefix_ref = refs[:parts], refs[-2], refs[-1]
     others = refs[-4:-2]
     size = prefix_ref.shape[1]
     local = gain_ref.shape[0] // parts
     block = 1 - me_ref[1]
-    for slot, slot_ref in enumerate(slots):
+    for slot, slot_ref in zip(order, slots):
         owner = me_ref[0] ^ slot
         prefix_ref[owner] = slot_ref[pl.ds(pl.multiple_of(block * size, size), size), :]
         if slot_ref.shape[0] > 2 * size:
@@ -489,15 +489,18 @@
     gain_type = jax.ShapeDtypeStruct((parts * local, dim), jnp.float32)
 
     def merge(group, before, cost):
+        order = list(range(parts))
+        if group == GROUPS - 1:
+            order = [0] + order[2:] + [1]
         return kernel_call(
-            functools.partial(merge_kernel, parts),
+            functools.partial(merge_kernel, parts, order),
             f"merge{group}",
             [vmem] * parts + [hbm] * len(before),
             [vmem] * 3,
             [half_type, half_type, gain_type],
             [pltpu.VMEM(part_type.shape, part_type.dtype)],
             cost=cost,
-        )(me, *prefixes[group], *before)
+        )(me, *(prefixes[group][slot] for slot in order), *before)
 
     def output(group, other, masks, received, out, before, cost=0):
         *out, made = kernel_call(
@@ -523,17 +526,12 @@
     for group in range(GROUPS):
         last = group == GROUPS - 1
         slots = prefixes[group]
-        if last:
-            out, before = output(group, 0, (0,), slots[:2], out, before)
         *others, came = merge(group, before, 0)
         if group == 0:
             gains = came
         others = [lax.ppermute(other, "core", swap) for other in others]
         before = (came,)
-        if last:
-            out, before = output(group, 0, (1,), slots[2:], out, before, cost=20)
-        else:
-            out, before = output(group, 0, (0, 1), slots, out, before)
+        out, before = output(group, 0, (0, 1), slots, out, before, cost=20 if last else 0)
         out, before = output(group, 1, (0, 1), others, out, before)
     return out[0]
 

time: 75.9 us -> 76.8 us (1.012)
  starting transfers between devices: 28.1 us -> 29.1 us
  Pallas kernels: 31.9 us -> 31.1 us
    ppermute x4, waiting for transfers between devices: 6.12 us -> 7.59 us  [with_plane(): return lax.ppermute(total, 'z', pairs)]
    pallas_call x5 -> x4, Pallas kernels: 10 us -> 8.76 us  [output(): kernel_call(functools.partial(output_kernel, dim, owned, half, group * sh...]
    ppermute x12, starting transfers between devices: 13.4 us -> 14.2 us  [exchange(): arrived[slot] = lax.ppermute(slots[slot], 'head', pairs)]
    ppermute x12, waiting for transfers between devices: 6.02 us -> 5.23 us  [exchange(): arrived[slot] = lax.ppermute(slots[slot], 'head', pairs)]
  transfers between devices with their start and end apart: 23 -> 23, of which waited for: 9 -> 8; matrix products, arithmetic and copies ran while one was open for 0% -> 0% of each run, Pallas kernels for 34% -> 33%
where the time goes in v2:
time: 76.8 us; the launch traced here: 76.4 us
  Pallas kernels  31.1 us (40%)
  starting transfers between devices  29.1 us (38%)
  waiting for transfers between devices  15.1 us (20%)
  local copies, waits for them, and re-layouts  0.86 us (1%)
    ppermute x12, starting transfers between devices, exchange(): arrived[slot] = lax.ppermute(slots[slot], 'head', pairs)  14.2 us
    pallas_call x4, Pallas kernels, output(): kernel_call(functools.partial(output_kernel, dim, owned, half, group * sh...  8.76 us
    ppermute x4, starting transfers between devices, with_plane(): return lax.ppermute(total, 'z', pairs)  8.07 us
    ppermute x4, waiting for transfers between devices, with_plane(): return lax.ppermute(total, 'z', pairs)  7.59 us
    pallas_call x4, Pallas kernels, inside_part(): kernel_call(functools.partial(inside_kernel, dim, half, group * share, sh...  7.01 us
    pallas_call x2, Pallas kernels, on_device(): kernel_call(functools.partial(state_kernel, dim, owned, half, group * sha...  6.03 us
    ppermute x12, waiting for transfers between devices, exchange(): arrived[slot] = lax.ppermute(slots[slot], 'head', pairs)  5.23 us
    all_to_all x1, starting transfers between devices, on_device(): decay = lax.all_to_all(packed, ('core', 'head'), 0, 0, tiled=True)  5.17 us
  transfers between devices with their start and end apart: 23, of which 8 were waited for; matrix products, arithmetic and copies ran while one was open for 0% of the time, Pallas kernels for 33%

profile of v2, /device:TPU:0, one launch (start us, length us, event | category | flops | bytes accessed | tf_op | source)
XLA Modules:
  0.0 76.4 jit_solution(12394246515477299019)
XLA Ops:
  0.5 1.4 %pack.1.refs_2_ = f32[8,16,128]{2,1,0:T(8,128)} custom-call(f32[1,16,512]{2,1,0:T(8,128)} %decay_ref.1), custom_call_target="tpu_custom_call" | custom-call | tf_op jit(solution)/shard_map/pack/pallas_call | solution.py:347
  1.9 5.2 %all-to-all-start = ((f32[8,16,128]{2,1,0:T(8,128)}), f32[8,16,128]{2,1,0:T(8,128)S(1)}, u32[]{:S(2)}, u32[]{:S(2)}) async-start(f32[8,16,128]{2,1,0:T(8,128)} %pack.1.refs_2_), calls=%async_computation | async-start | bytes 131072 | tf_op jit(solution)/shard_map/all_to_all | solution.py:352
  8.0 1.8 %load.1 = (bf16[128,2048]{1,0:T(8,128)(2,1)S(1)}, bf16[128,2048]{1,0:T(8,128)(2,1)S(1)}) custom-call(s32[3]{0:T(128)S(1)} %pad_add_fusion.me_ref, bf16[1,128,8192]{2,1,0:T(8,128)(2,1)} %keys_ref.7, bf16[1,128,8192]{2,1,0:T(8,128)(2,1)} %values_ref.7, f32[8,16,128]{2,1,0:T(8,128)S(1)} %copy-done.4), custom_call_target="tpu_custom_call" | custom-call | flops 1 | bytes 1 | tf_op jit(solution)/shard_map/load/pallas_call | solution.py:398
  9.8 2.2 %all-to-all-done.decay_ref = f32[8,16,128]{2,1,0:T(8,128)S(1)} async-done(((f32[8,16,128]{2,1,0:T(8,128)}), f32[8,16,128]{2,1,0:T(8,128)S(1)}, u32[]{:S(2)}, u32[]{:S(2)}) %all-to-all-start) | async-done | bytes 65568 | tf_op jit(solution)/shard_map/all_to_all | solution.py:352
  12.0 2.7 %state0.1 = (bf16[2,528,128]{2,1,0:T(8,128)(2,1)S(1)}, bf16[2,528,128]{2,1,0:T(8,128)(2,1)S(1)}, bf16[2,528,128]{2,1,0:T(8,128)(2,1)S(1)}, bf16[2,528,128]{2,1,0:T(8,128)(2,1)S(1)}) custom-call(s32[3]{0:T(128)S(1)} %pad_add_fusion.me_ref, f32[8,16,128]{2,1,0:T(8,128)S(1)} %all-to-all-done.decay_ref, bf16[128,2048]{1,0:T(8,128)(2,1)S(1)} %get-tuple-element.52.refs_0_, ...), custom_call_target="tpu_custom_call" | custom-call | flops 1 | bytes 1 | tf_op jit(solution)/shard_map/state0/pallas_call | solution.py:410
  15.3 1.5 %collective-permute-start.7 = (bf16[2,528,128]{2,1,0:T(8,128)(2,1)S(1)}, bf16[2,528,128]{2,1,0:T(8,128)(2,1)S(1)}, u32[]{:S(2)}, u32[]{:S(2)}) collective-permute-start(bf16[2,528,128]{2,1,0:T(8,128)(2,1)S(1)} %get-tuple-element.61), channel_id=1, source_target_pairs={{0,24},{8,16},{16,8},{24,0},{1,25},{9,17},{17,9},{25,1},{2,26},{10... | collective-permute-start | bytes 811016 | tf_op jit(solution)/shard_map/ppermute | solution.py:372
  16.9 1.4 %collective-permute-start.6 = (bf16[2,528,128]{2,1,0:T(8,128)(2,1)S(1)}, bf16[2,528,128]{2,1,0:T(8,128)(2,1)S(1)}, u32[]{:S(2)}, u32[]{:S(2)}) collective-permute-start(bf16[2,528,128]{2,1,0:T(8,128)(2,1)S(1)} %get-tuple-element.54.refs_4_), channel_id=1, source_target_pairs={{0,16},{8,24},{16,0},{24,8},{1,17},{9,25},{17,1},{25,9},{2,18},{10... | collective-permute-start | bytes 811016 | tf_op jit(solution)/shard_map/ppermute | solution.py:372
  18.3 3.4 %state1.1 = (bf16[2,528,128]{2,1,0:T(8,128)(2,1)S(1)}, bf16[2,528,128]{2,1,0:T(8,128)(2,1)S(1)}, bf16[2,528,128]{2,1,0:T(8,128)(2,1)S(1)}, bf16[2,528,128]{2,1,0:T(8,128)(2,1)S(1)}) custom-call(s32[3]{0:T(128)S(1)} %pad_add_fusion.me_ref, f32[8,16,128]{2,1,0:T(8,128)S(1)} %all-to-all-done.decay_ref, bf16[1,128,8192]{2,1,0:T(8,128)(2,1)} %keys_ref.7, ...), custom_call_target="tpu_custom_call" | custom-call | flops 1 | bytes 1 | tf_op jit(solution)/shard_map/state1/pallas_call | solution.py:410
  22.4 1.6 %collective-permute-start.4 = (bf16[2,528,128]{2,1,0:T(8,128)(2,1)S(1)}, bf16[2,528,128]{2,1,0:T(8,128)(2,1)S(1)}, u32[]{:S(2)}, u32[]{:S(2)}) collective-permute-start(bf16[2,528,128]{2,1,0:T(8,128)(2,1)S(1)} %get-tuple-element.58), channel_id=1, source_target_pairs={{0,24},{8,16},{16,8},{24,0},{1,25},{9,17},{17,9},{25,1},{2,26},{10... | collective-permute-start | bytes 811016 | tf_op jit(solution)/shard_map/ppermute | solution.py:372
  24.1 1.2 %collective-permute-start.3 = (bf16[2,528,128]{2,1,0:T(8,128)(2,1)S(1)}, bf16[2,528,128]{2,1,0:T(8,128)(2,1)S(1)}, u32[]{:S(2)}, u32[]{:S(2)}) collective-permute-start(bf16[2,528,128]{2,1,0:T(8,128)(2,1)S(1)} %get-tuple-element.57.rest_0_), channel_id=1, source_target_pairs={{0,16},{8,24},{16,0},{24,8},{1,17},{9,25},{17,1},{25,9},{2,18},{10... | collective-permute-start | bytes 811016 | tf_op jit(solution)/shard_map/ppermute | solution.py:372
  25.3 1.8 %inside0_0.1 = (f32[128,2048]{1,0:T(8,128)S(1)}, f32[2,128,8]{2,1,0:T(8,128)S(1)}, f32[128,2048]{1,0:T(8,128)S(1)}, f32[8,128]{1,0:T(8,128)S(1)}) custom-call(s32[3]{0:T(128)S(1)} %pad_add_fusion.me_ref, bf16[1,128,8192]{2,1,0:T(8,128)(2,1)S(1)} %copy-done, bf16[1,128,8192]{2,1,0:T(8,128)(2,1)S(1)} %copy-done.1, bf16[1,128,8192]{2,1,0:T(8,128)(2,1)S(1)} %copy-done.2, ...), custom_call_target="tpu_custom_call" | custom-call | flops 1 | bytes 1 | tf_op jit(solution)/shard_map/inside0_0/pallas_call | solution.py:383
  27.0 1.8 %inside0_1.1 = (f32[128,2048]{1,0:T(8,128)S(1)}, f32[2,128,8]{2,1,0:T(8,128)S(1)}, f32[128,2048]{1,0:T(8,128)S(1)}, f32[8,128]{1,0:T(8,128)S(1)}) custom-call(s32[3]{0:T(128)S(1)} %pad_add_fusion.me_ref, bf16[1,128,8192]{2,1,0:T(8,128)(2,1)S(1)} %copy-done, bf16[1,128,8192]{2,1,0:T(8,128)(2,1)S(1)} %copy-done.1, bf16[1,128,8192]{2,1,0:T(8,128)(2,1)S(1)} %copy-done.2, ...), custom_call_target="tpu_custom_call" | custom-call | flops 1 | bytes 1 | tf_op jit(solution)/shard_map/inside0_1/pallas_call | solution.py:383
  28.8 1.2 %collective-permute-done.7.refs_3_ = bf16[2,528,128]{2,1,0:T(8,128)(2,1)S(1)} collective-permute-done((bf16[2,528,128]{2,1,0:T(8,128)(2,1)S(1)}, bf16[2,528,128]{2,1,0:T(8,128)(2,1)S(1)}, u32[]{:S(2)}, u32[]{:S(2)}) %collective-permute-start.7) | collective-permute-done | bytes 270368 | tf_op jit(solution)/shard_map/ppermute | solution.py:372
  30.0 1.8 %collective-permute-done.6.refs_2_ = bf16[2,528,128]{2,1,0:T(8,128)(2,1)S(1)} collective-permute-done((bf16[2,528,128]{2,1,0:T(8,128)(2,1)S(1)}, bf16[2,528,128]{2,1,0:T(8,128)(2,1)S(1)}, u32[]{:S(2)}, u32[]{:S(2)}) %collective-permute-start.6) | collective-permute-done | bytes 270368 | tf_op jit(solution)/shard_map/ppermute | solution.py:372
  32.7 1.6 %collective-permute-start.8 = (bf16[528,128]{1,0:T(8,128)(2,1)S(1)}, bf16[528,128]{1,0:T(8,128)(2,1)S(1)}, u32[]{:S(2)}, u32[]{:S(2)}) collective-permute-start(bf16[528,128]{1,0:T(8,128)(2,1)S(1)} %total0.1.rest_0_.mine_ref), channel_id=1, source_target_pairs={{0,2},{2,0},{4,6},{6,4},{1,3},{3,1},{5,7},{7,5},{8,10},{10,8},{12,... | collective-permute-start | bytes 405512 | tf_op jit(solution)/shard_map/ppermute | solution.py:434
  34.4 1.7 %inside1_0.1 = (f32[128,2048]{1,0:T(8,128)S(1)}, f32[2,128,8]{2,1,0:T(8,128)S(1)}, f32[128,2048]{1,0:T(8,128)S(1)}, f32[8,128]{1,0:T(8,128)S(1)}) custom-call(s32[3]{0:T(128)S(1)} %pad_add_fusion.me_ref, bf16[1,128,8192]{2,1,0:T(8,128)(2,1)S(1)} %copy-done, bf16[1,128,8192]{2,1,0:T(8,128)(2,1)S(1)} %copy-done.1, bf16[1,128,8192]{2,1,0:T(8,128)(2,1)S(1)} %copy-done.2, ...), custom_call_target="tpu_custom_call" | custom-call | flops 1 | bytes 1 | tf_op jit(solution)/shard_map/inside1_0/pallas_call | solution.py:383
  36.1 3.0 %collective-permute-done.8.other_ref.refs_4_ = bf16[528,128]{1,0:T(8,128)(2,1)S(1)} collective-permute-done((bf16[528,128]{1,0:T(8,128)(2,1)S(1)}, bf16[528,128]{1,0:T(8,128)(2,1)S(1)}, u32[]{:S(2)}, u32[]{:S(2)}) %collective-permute-start.8) | collective-permute-done | bytes 135200 | tf_op jit(solution)/shard_map/ppermute | solution.py:434
  39.8 2.7 %collective-permute-start.10 = (bf16[528,128]{1,0:T(8,128)(2,1)S(1)}, bf16[528,128]{1,0:T(8,128)(2,1)S(1)}, u32[]{:S(2)}, u32[]{:S(2)}) collective-permute-start(bf16[528,128]{1,0:T(8,128)(2,1)S(1)} %widen0_0.1.refs_4_), channel_id=1, source_target_pairs={{0,4},{2,6},{4,0},{6,2},{1,5},{3,7},{5,1},{7,3},{8,12},{10,14},{12... | collective-permute-start | bytes 405512 | tf_op jit(solution)/shard_map/ppermute | solution.py:434
  43.4 1.2 %collective-permute-start.9 = (bf16[528,128]{1,0:T(8,128)(2,1)S(1)}, bf16[528,128]{1,0:T(8,128)(2,1)S(1)}, u32[]{:S(2)}, u32[]{:S(2)}) collective-permute-start(bf16[528,128]{1,0:T(8,128)(2,1)S(1)} %total1.1.refs_6_.mine_ref), channel_id=1, source_target_pairs={{0,2},{2,0},{4,6},{6,4},{1,3},{3,1},{5,7},{7,5},{8,10},{10,8},{12,... | collective-permute-start | bytes 405512 | tf_op jit(solution)/shard_map/ppermute | solution.py:434
  44.6 2.7 %collective-permute-done.10.refs_5_ = bf16[528,128]{1,0:T(8,128)(2,1)S(1)} collective-permute-done((bf16[528,128]{1,0:T(8,128)(2,1)S(1)}, bf16[528,128]{1,0:T(8,128)(2,1)S(1)}, u32[]{:S(2)}, u32[]{:S(2)}) %collective-permute-start.10) | collective-permute-done | bytes 135200 | tf_op jit(solution)/shard_map/ppermute | solution.py:434
  48.8 1.4 %collective-permute-start.12 = (bf16[1040,128]{1,0:T(8,128)(2,1)S(1)}, bf16[1040,128]{1,0:T(8,128)(2,1)S(1)}, u32[]{:S(2)}, u32[]{:S(2)}) collective-permute-start(bf16[1040,128]{1,0:T(8,128)(2,1)S(1)} %get-tuple-element.70), channel_id=1, source_target_pairs={{0,16},{8,24},{16,0},{24,8},{1,17},{9,25},{17,1},{25,9},{2,18},{10... | collective-permute-start | bytes 798728 | tf_op jit(solution)/shard_map/ppermute | solution.py:372
  50.3 1.5 %collective-permute-start.13 = (bf16[1040,128]{1,0:T(8,128)(2,1)S(1)}, bf16[1040,128]{1,0:T(8,128)(2,1)S(1)}, u32[]{:S(2)}, u32[]{:S(2)}) collective-permute-start(bf16[1040,128]{1,0:T(8,128)(2,1)S(1)} %get-tuple-element.71), channel_id=1, source_target_pairs={{0,24},{8,16},{16,8},{24,0},{1,25},{9,17},{17,9},{25,1},{2,26},{10... | collective-permute-start | bytes 798728 | tf_op jit(solution)/shard_map/ppermute | solution.py:372
  52.4 2.5 %collective-permute-start.14 = (bf16[528,128]{1,0:T(8,128)(2,1)S(1)}, bf16[528,128]{1,0:T(8,128)(2,1)S(1)}, u32[]{:S(2)}, u32[]{:S(2)}) collective-permute-start(bf16[528,128]{1,0:T(8,128)(2,1)S(1)} %widen1_0.1.rest_0_), channel_id=1, source_target_pairs={{0,4},{2,6},{4,0},{6,2},{1,5},{3,7},{5,1},{7,3},{8,12},{10,14},{12... | collective-permute-start | bytes 405512 | tf_op jit(solution)/shard_map/ppermute | solution.py:434
  54.9 1.7 %inside1_1.1 = (f32[128,2048]{1,0:T(8,128)S(1)}, f32[2,128,8]{2,1,0:T(8,128)S(1)}, f32[128,2048]{1,0:T(8,128)S(1)}, f32[8,128]{1,0:T(8,128)S(1)}) custom-call(s32[3]{0:T(128)S(1)} %pad_add_fusion.me_ref, bf16[1,128,8192]{2,1,0:T(8,128)(2,1)S(1)} %copy-done, bf16[1,128,8192]{2,1,0:T(8,128)(2,1)S(1)} %copy-done.1, bf16[1,128,8192]{2,1,0:T(8,128)(2,1)S(1)} %copy-done.2, ...), custom_call_target="tpu_custom_call" | custom-call | flops 2000000000 | bytes 1 | tf_op jit(solution)/shard_map/inside1_1/pallas_call | solution.py:383
  56.7 1.9 %collective-permute-done.14.refs_5_ = bf16[528,128]{1,0:T(8,128)(2,1)S(1)} collective-permute-done((bf16[528,128]{1,0:T(8,128)(2,1)S(1)}, bf16[528,128]{1,0:T(8,128)(2,1)S(1)}, u32[]{:S(2)}, u32[]{:S(2)}) %collective-permute-start.14) | collective-permute-done | bytes 135200 | tf_op jit(solution)/shard_map/ppermute | solution.py:434
  59.6 1.4 %collective-permute-start.15 = (bf16[1040,128]{1,0:T(8,128)(2,1)S(1)}, bf16[1040,128]{1,0:T(8,128)(2,1)S(1)}, u32[]{:S(2)}, u32[]{:S(2)}) collective-permute-start(bf16[1040,128]{1,0:T(8,128)(2,1)S(1)} %get-tuple-element.75), channel_id=1, source_target_pairs={{0,16},{8,24},{16,0},{24,8},{1,17},{9,25},{17,1},{25,9},{2,18},{10... | collective-permute-start | bytes 798728 | tf_op jit(solution)/shard_map/ppermute | solution.py:372
  61.5 1.6 %collective-permute-start.17 = (bf16[1040,128]{1,0:T(8,128)(2,1)S(1)}, bf16[1040,128]{1,0:T(8,128)(2,1)S(1)}, u32[]{:S(2)}, u32[]{:S(2)}) collective-permute-start(bf16[1040,128]{1,0:T(8,128)(2,1)S(1)} %get-tuple-element.77), channel_id=1, source_target_pairs={{0,8},{8,0},{16,24},{24,16},{1,9},{9,1},{17,25},{25,17},{2,10},{10... | collective-permute-start | bytes 798728 | tf_op jit(solution)/shard_map/ppermute | solution.py:372
  64.3 2.1 %output0_0_0.1 = (bf16[1,128,8192]{2,1,0:T(8,128)(2,1)}, f32[8,128]{1,0:T(8,128)S(1)}) custom-call(s32[3]{0:T(128)S(1)} %pad_add_fusion.me_ref, bf16[1,128,8192]{2,1,0:T(8,128)(2,1)S(1)} %copy-done, f32[128,2048]{1,0:T(8,128)S(1)} %get-tuple-element.83.inside_ref, f32[2,128,8]{2,1,0:T(8,128)S(1)} %get-tuple-element.84.down_ref, ...), custom_call_target="tpu_custom_call" | custom-call | flops 1 | bytes 1 | tf_op jit(solution)/shard_map/output0_0_0/pallas_call | solution.py:506
  66.4 2.0 %output0_1_0.1 = (bf16[1,128,8192]{2,1,0:T(8,128)(2,1)}, f32[8,128]{1,0:T(8,128)S(1)}) custom-call(s32[3]{0:T(128)S(1)} %pad_add_fusion.me_ref, bf16[1,128,8192]{2,1,0:T(8,128)(2,1)S(1)} %copy-done, f32[128,2048]{1,0:T(8,128)S(1)} %get-tuple-element.78.inside_ref, f32[2,128,8]{2,1,0:T(8,128)S(1)} %get-tuple-element.79.down_ref, ...), custom_call_target="tpu_custom_call", output_to_operand_aliasing={{0}: (8, {})} | custom-call | flops 1 | bytes 1 | tf_op jit(solution)/shard_map/output0_1_0/pallas_call | solution.py:506
  68.4 2.0 %collective-permute-done.15.refs_1_.refs_2_ = bf16[1040,128]{1,0:T(8,128)(2,1)S(1)} collective-permute-done((bf16[1040,128]{1,0:T(8,128)(2,1)S(1)}, bf16[1040,128]{1,0:T(8,128)(2,1)S(1)}, u32[]{:S(2)}, u32[]{:S(2)}) %collective-permute-start.15) | collective-permute-done | bytes 266272 | tf_op jit(solution)/shard_map/ppermute | solution.py:372
  71.7 2.1 %output1_0_0.1 = (bf16[1,128,8192]{2,1,0:T(8,128)(2,1)}, f32[8,128]{1,0:T(8,128)S(1)}) custom-call(s32[3]{0:T(128)S(1)} %pad_add_fusion.me_ref, bf16[1,128,8192]{2,1,0:T(8,128)(2,1)S(1)} %copy-done, f32[128,2048]{1,0:T(8,128)S(1)} %get-tuple-element.91.inside_ref, f32[2,128,8]{2,1,0:T(8,128)S(1)} %get-tuple-element.92.down_ref, ...), custom_call_target="tpu_custom_call", output_to_operand_aliasing={{0}: (10, {})} | custom-call | flops 20000000000 | bytes 1 | tf_op jit(solution)/shard_map/output1_0_0/pallas_call | solution.py:506
  73.8 2.6 %output1_1_0.1 = (bf16[1,128,8192]{2,1,0:T(8,128)(2,1)}, f32[8,128]{1,0:T(8,128)}) custom-call(s32[3]{0:T(128)S(1)} %pad_add_fusion.me_ref, bf16[1,128,8192]{2,1,0:T(8,128)(2,1)S(1)} %copy-done, f32[128,2048]{1,0:T(8,128)S(1)} %get-tuple-element.66.inside_ref, f32[2,128,8]{2,1,0:T(8,128)S(1)} %get-tuple-element.67.down_ref, ...), custom_call_target="tpu_custom_call", output_to_operand_aliasing={{0}: (8, {})} | custom-call | flops 1 | bytes 1 | tf_op jit(solution)/shard_map/output1_1_0/pallas_call | solution.py:506
  (47 shorter events, 11.3 us)
Async XLA Ops:
  0.0 12.0 %collective-permute-start = (bf16[1,128,8192]{2,1,0:T(8,128)(2,1)}, bf16[1,128,8192]{2,1,0:T(8,128)(2,1)S(1)}, u32[]{:S(2)}, u32[]{:S(2)}) collective-permute-start(bf16[1,128,8192]{2,1,0:T(8,128)(2,1)} %keys_ref.7), channel_id=1, source_target_pairs={{0,1},{1,0},{2,3},{3,2},{4,5},{5,4},{6,7},{7,6},{8,9},{9,8},{10,11... | collective-permute-start | bytes 6291464 | tf_op jit(solution)/shard_map/ppermute | solution.py:346
  0.5 11.6 %collective-permute-start.1 = (bf16[1,128,8192]{2,1,0:T(8,128)(2,1)}, bf16[1,128,8192]{2,1,0:T(8,128)(2,1)}, u32[]{:S(2)}, u32[]{:S(2)}) collective-permute-start(bf16[1,128,8192]{2,1,0:T(8,128)(2,1)} %values_ref.7), channel_id=1, source_target_pairs={{0,1},{1,0},{2,3},{3,2},{4,5},{5,4},{6,7},{7,6},{8,9},{9,8},{10,11... | collective-permute-start | bytes 6291464 | tf_op jit(solution)/shard_map/ppermute | solution.py:345
  1.9 10.1 %all-to-all-start = ((f32[8,16,128]{2,1,0:T(8,128)}), f32[8,16,128]{2,1,0:T(8,128)S(1)}, u32[]{:S(2)}, u32[]{:S(2)}) async-start(f32[8,16,128]{2,1,0:T(8,128)} %pack.1.refs_2_), calls=%async_computation | async-start | bytes 131072 | tf_op jit(solution)/shard_map/all_to_all | solution.py:352
  7.1 0.8 %copy-start.4 = (f32[8,16,128]{2,1,0:T(8,128)S(1)}, f32[8,16,128]{2,1,0:T(8,128)}, u32[]{:S(2)}) copy-start(f32[8,16,128]{2,1,0:T(8,128)} %pack.1.refs_2_) | copy-start | bytes 196612
  14.7 9.4 %collective-permute-start.5 = (bf16[2,528,128]{2,1,0:T(8,128)(2,1)S(1)}, bf16[2,528,128]{2,1,0:T(8,128)(2,1)S(1)}, u32[]{:S(2)}, u32[]{:S(2)}) collective-permute-start(bf16[2,528,128]{2,1,0:T(8,128)(2,1)S(1)} %get-tuple-element.60), channel_id=1, source_target_pairs={{0,8},{8,0},{16,24},{24,16},{1,9},{9,1},{17,25},{25,17},{2,10},{10... | collective-permute-start | bytes 811016 | tf_op jit(solution)/shard_map/ppermute | solution.py:372
  15.3 14.7 %collective-permute-start.7 = (bf16[2,528,128]{2,1,0:T(8,128)(2,1)S(1)}, bf16[2,528,128]{2,1,0:T(8,128)(2,1)S(1)}, u32[]{:S(2)}, u32[]{:S(2)}) collective-permute-start(bf16[2,528,128]{2,1,0:T(8,128)(2,1)S(1)} %get-tuple-element.61), channel_id=1, source_target_pairs={{0,24},{8,16},{16,8},{24,0},{1,25},{9,17},{17,9},{25,1},{2,26},{10... | collective-permute-start | bytes 811016 | tf_op jit(solution)/shard_map/ppermute | solution.py:372
  16.9 8.4 %copy-start = (bf16[1,128,8192]{2,1,0:T(8,128)(2,1)S(1)}, bf16[1,128,8192]{2,1,0:T(8,128)(2,1)}, u32[]{:S(2)}) copy-start(bf16[1,128,8192]{2,1,0:T(8,128)(2,1)} %queries_ref.15) | copy-start | bytes 6291460
  16.9 8.4 %copy-start.1 = (bf16[1,128,8192]{2,1,0:T(8,128)(2,1)S(1)}, bf16[1,128,8192]{2,1,0:T(8,128)(2,1)}, u32[]{:S(2)}) copy-start(bf16[1,128,8192]{2,1,0:T(8,128)(2,1)} %keys_ref.7) | copy-start | bytes 6291460
  16.9 8.4 %copy-start.2 = (bf16[1,128,8192]{2,1,0:T(8,128)(2,1)S(1)}, bf16[1,128,8192]{2,1,0:T(8,128)(2,1)}, u32[]{:S(2)}) copy-start(bf16[1,128,8192]{2,1,0:T(8,128)(2,1)} %values_ref.7) | copy-start | bytes 6291460
  16.9 8.4 %copy-start.3 = (bf16[1,128,8192]{2,1,0:T(8,128)(2,1)S(1)}, bf16[1,128,8192]{2,1,0:T(8,128)(2,1)}, u32[]{:S(2)}) copy-start(bf16[1,128,8192]{2,1,0:T(8,128)(2,1)} %gate_ref.7) | copy-start | bytes 6291460
  16.9 15.0 %collective-permute-start.6 = (bf16[2,528,128]{2,1,0:T(8,128)(2,1)S(1)}, bf16[2,528,128]{2,1,0:T(8,128)(2,1)S(1)}, u32[]{:S(2)}, u32[]{:S(2)}) collective-permute-start(bf16[2,528,128]{2,1,0:T(8,128)(2,1)S(1)} %get-tuple-element.54.refs_4_), channel_id=1, source_target_pairs={{0,16},{8,24},{16,0},{24,8},{1,17},{9,25},{17,1},{25,9},{2,18},{10... | collective-permute-start | bytes 811016 | tf_op jit(solution)/shard_map/ppermute | solution.py:372
  21.7 20.8 %collective-permute-start.2 = (bf16[2,528,128]{2,1,0:T(8,128)(2,1)S(1)}, bf16[2,528,128]{2,1,0:T(8,128)(2,1)S(1)}, u32[]{:S(2)}, u32[]{:S(2)}) collective-permute-start(bf16[2,528,128]{2,1,0:T(8,128)(2,1)S(1)} %get-tuple-element.56), channel_id=1, source_target_pairs={{0,8},{8,0},{16,24},{24,16},{1,9},{9,1},{17,25},{25,17},{2,10},{10... | collective-permute-start | bytes 811016 | tf_op jit(solution)/shard_map/ppermute | solution.py:372
  22.4 20.2 %collective-permute-start.4 = (bf16[2,528,128]{2,1,0:T(8,128)(2,1)S(1)}, bf16[2,528,128]{2,1,0:T(8,128)(2,1)S(1)}, u32[]{:S(2)}, u32[]{:S(2)}) collective-permute-start(bf16[2,528,128]{2,1,0:T(8,128)(2,1)S(1)} %get-tuple-element.58), channel_id=1, source_target_pairs={{0,24},{8,16},{16,8},{24,0},{1,25},{9,17},{17,9},{25,1},{2,26},{10... | collective-permute-start | bytes 811016 | tf_op jit(solution)/shard_map/ppermute | solution.py:372
  24.1 18.5 %collective-permute-start.3 = (bf16[2,528,128]{2,1,0:T(8,128)(2,1)S(1)}, bf16[2,528,128]{2,1,0:T(8,128)(2,1)S(1)}, u32[]{:S(2)}, u32[]{:S(2)}) collective-permute-start(bf16[2,528,128]{2,1,0:T(8,128)(2,1)S(1)} %get-tuple-element.57.rest_0_), channel_id=1, source_target_pairs={{0,16},{8,24},{16,0},{24,8},{1,17},{9,25},{17,1},{25,9},{2,18},{10... | collective-permute-start | bytes 811016 | tf_op jit(solution)/shard_map/ppermute | solution.py:372
  32.7 14.5 %copy-start.5 = (bf16[2048]{0:T(1024)(128)(2,1)S(1)}, bf16[2048]{0:T(1024)(128)(2,1)}, u32[]{:S(2)}) copy-start(bf16[2048]{0:T(1024)(128)(2,1)} %param.11) | copy-start | bytes 12292
  32.7 6.4 %collective-permute-start.8 = (bf16[528,128]{1,0:T(8,128)(2,1)S(1)}, bf16[528,128]{1,0:T(8,128)(2,1)S(1)}, u32[]{:S(2)}, u32[]{:S(2)}) collective-permute-start(bf16[528,128]{1,0:T(8,128)(2,1)S(1)} %total0.1.rest_0_.mine_ref), channel_id=1, source_target_pairs={{0,2},{2,0},{4,6},{6,4},{1,3},{3,1},{5,7},{7,5},{8,10},{10,8},{12,... | collective-permute-start | bytes 405512 | tf_op jit(solution)/shard_map/ppermute | solution.py:434
  39.8 7.5 %collective-permute-start.10 = (bf16[528,128]{1,0:T(8,128)(2,1)S(1)}, bf16[528,128]{1,0:T(8,128)(2,1)S(1)}, u32[]{:S(2)}, u32[]{:S(2)}) collective-permute-start(bf16[528,128]{1,0:T(8,128)(2,1)S(1)} %widen0_0.1.refs_4_), channel_id=1, source_target_pairs={{0,4},{2,6},{4,0},{6,2},{1,5},{3,7},{5,1},{7,3},{8,12},{10,14},{12... | collective-permute-start | bytes 405512 | tf_op jit(solution)/shard_map/ppermute | solution.py:434
  43.4 8.4 %collective-permute-start.9 = (bf16[528,128]{1,0:T(8,128)(2,1)S(1)}, bf16[528,128]{1,0:T(8,128)(2,1)S(1)}, u32[]{:S(2)}, u32[]{:S(2)}) collective-permute-start(bf16[528,128]{1,0:T(8,128)(2,1)S(1)} %total1.1.refs_6_.mine_ref), channel_id=1, source_target_pairs={{0,2},{2,0},{4,6},{6,4},{1,3},{3,1},{5,7},{7,5},{8,10},{10,8},{12,... | collective-permute-start | bytes 405512 | tf_op jit(solution)/shard_map/ppermute | solution.py:434
  48.2 13.3 %collective-permute-start.11 = (bf16[1040,128]{1,0:T(8,128)(2,1)S(1)}, bf16[1040,128]{1,0:T(8,128)(2,1)S(1)}, u32[]{:S(2)}, u32[]{:S(2)}) collective-permute-start(bf16[1040,128]{1,0:T(8,128)(2,1)S(1)} %get-tuple-element.69), channel_id=1, source_target_pairs={{0,8},{8,0},{16,24},{24,16},{1,9},{9,1},{17,25},{25,17},{2,10},{10... | collective-permute-start | bytes 798728 | tf_op jit(solution)/shard_map/ppermute | solution.py:372
  48.8 14.3 %collective-permute-start.12 = (bf16[1040,128]{1,0:T(8,128)(2,1)S(1)}, bf16[1040,128]{1,0:T(8,128)(2,1)S(1)}, u32[]{:S(2)}, u32[]{:S(2)}) collective-permute-start(bf16[1040,128]{1,0:T(8,128)(2,1)S(1)} %get-tuple-element.70), channel_id=1, source_target_pairs={{0,16},{8,24},{16,0},{24,8},{1,17},{9,25},{17,1},{25,9},{2,18},{10... | collective-permute-start | bytes 798728 | tf_op jit(solution)/shard_map/ppermute | solution.py:372
  50.3 12.9 %collective-permute-start.13 = (bf16[1040,128]{1,0:T(8,128)(2,1)S(1)}, bf16[1040,128]{1,0:T(8,128)(2,1)S(1)}, u32[]{:S(2)}, u32[]{:S(2)}) collective-permute-start(bf16[1040,128]{1,0:T(8,128)(2,1)S(1)} %get-tuple-element.71), channel_id=1, source_target_pairs={{0,24},{8,16},{16,8},{24,0},{1,25},{9,17},{17,9},{25,1},{2,26},{10... | collective-permute-start | bytes 798728 | tf_op jit(solution)/shard_map/ppermute | solution.py:372
  52.4 6.2 %collective-permute-start.14 = (bf16[528,128]{1,0:T(8,128)(2,1)S(1)}, bf16[528,128]{1,0:T(8,128)(2,1)S(1)}, u32[]{:S(2)}, u32[]{:S(2)}) collective-permute-start(bf16[528,128]{1,0:T(8,128)(2,1)S(1)} %widen1_0.1.rest_0_), channel_id=1, source_target_pairs={{0,4},{2,6},{4,0},{6,2},{1,5},{3,7},{5,1},{7,3},{8,12},{10,14},{12... | collective-permute-start | bytes 405512 | tf_op jit(solution)/shard_map/ppermute | solution.py:434
  59.6 10.9 %collective-permute-start.15 = (bf16[1040,128]{1,0:T(8,128)(2,1)S(1)}, bf16[1040,128]{1,0:T(8,128)(2,1)S(1)}, u32[]{:S(2)}, u32[]{:S(2)}) collective-permute-start(bf16[1040,128]{1,0:T(8,128)(2,1)S(1)} %get-tuple-element.75), channel_id=1, source_target_pairs={{0,16},{8,24},{16,0},{24,8},{1,17},{9,25},{17,1},{25,9},{2,18},{10... | collective-permute-start | bytes 798728 | tf_op jit(solution)/shard_map/ppermute | solution.py:372
  60.9 9.6 %collective-permute-start.16 = (bf16[1040,128]{1,0:T(8,128)(2,1)S(1)}, bf16[1040,128]{1,0:T(8,128)(2,1)S(1)}, u32[]{:S(2)}, u32[]{:S(2)}) collective-permute-start(bf16[1040,128]{1,0:T(8,128)(2,1)S(1)} %get-tuple-element.76), channel_id=1, source_target_pairs={{0,24},{8,16},{16,8},{24,0},{1,25},{9,17},{17,9},{25,1},{2,26},{10... | collective-permute-start | bytes 798728 | tf_op jit(solution)/shard_map/ppermute | solution.py:372
  61.5 9.0 %collective-permute-start.17 = (bf16[1040,128]{1,0:T(8,128)(2,1)S(1)}, bf16[1040,128]{1,0:T(8,128)(2,1)S(1)}, u32[]{:S(2)}, u32[]{:S(2)}) collective-permute-start(bf16[1040,128]{1,0:T(8,128)(2,1)S(1)} %get-tuple-element.77), channel_id=1, source_target_pairs={{0,8},{8,0},{16,24},{24,16},{1,9},{9,1},{17,25},{25,17},{2,10},{10... | collective-permute-start | bytes 798728 | tf_op jit(solution)/shard_map/ppermute | solution.py:372
  63.8 2.7 %collective-permute-start.18 = (bf16[2,512,128]{2,1,0:T(8,128)(2,1)S(1)}, bf16[2,512,128]{2,1,0:T(8,128)(2,1)S(1)}, u32[]{:S(2)}, u32[]{:S(2)}) collective-permute-start(bf16[2,512,128]{2,1,0:T(8,128)(2,1)S(1)} %get-tuple-element.81), channel_id=1, source_target_pairs={{0,1},{1,0},{2,3},{3,2},{4,5},{5,4},{6,7},{7,6},{8,9},{9,8},{10,11... | collective-permute-start | bytes 786440 | tf_op jit(solution)/shard_map/ppermute | solution.py:532
  63.8 2.6 %collective-permute-start.19 = (bf16[2,512,128]{2,1,0:T(8,128)(2,1)S(1)}, bf16[2,512,128]{2,1,0:T(8,128)(2,1)S(1)}, u32[]{:S(2)}, u32[]{:S(2)}) collective-permute-start(bf16[2,512,128]{2,1,0:T(8,128)(2,1)S(1)} %get-tuple-element.82), channel_id=1, source_target_pairs={{0,1},{1,0},{2,3},{3,2},{4,5},{5,4},{6,7},{7,6},{8,9},{9,8},{10,11... | collective-permute-start | bytes 786440 | tf_op jit(solution)/shard_map/ppermute | solution.py:532
  71.1 2.7 %collective-permute-start.20 = (bf16[2,512,128]{2,1,0:T(8,128)(2,1)S(1)}, bf16[2,512,128]{2,1,0:T(8,128)(2,1)S(1)}, u32[]{:S(2)}, u32[]{:S(2)}) collective-permute-start(bf16[2,512,128]{2,1,0:T(8,128)(2,1)S(1)} %get-tuple-element.89), channel_id=1, source_target_pairs={{0,1},{1,0},{2,3},{3,2},{4,5},{5,4},{6,7},{7,6},{8,9},{9,8},{10,11... | collective-permute-start | bytes 786440 | tf_op jit(solution)/shard_map/ppermute | solution.py:532
  71.2 2.6 %collective-permute-start.21 = (bf16[2,512,128]{2,1,0:T(8,128)(2,1)S(1)}, bf16[2,512,128]{2,1,0:T(8,128)(2,1)S(1)}, u32[]{:S(2)}, u32[]{:S(2)}) collective-permute-start(bf16[2,512,128]{2,1,0:T(8,128)(2,1)S(1)} %get-tuple-element.90), channel_id=1, source_target_pairs={{0,1},{1,0},{2,3},{3,2},{4,5},{5,4},{6,7},{7,6},{8,9},{9,8},{10,11... | collective-permute-start | bytes 786440 | tf_op jit(solution)/shard_map/ppermute | solution.py:532
